TPU v7x, 256 devices: a whole 4x4x8 slice. The times are simulated.
256 devices in a mesh: token: 16 (over x_lo, y, core), brow: 8 (over z), bcol: 2 (over x_hi).
Axes of the slice: x: 4 (x_hi: 2, x_lo: 2; x = x_hi * 2 + x_lo), y: 4, z: 8, core: 2. Of those that a mesh axis runs over, the one named last changes fastest.
Arguments:
- layer_input: bfloat16 [16384, 8192], P('token', ('brow', 'bcol')), may hold values from -6 to 6
- pairs: int32 [2, 16, 32], P(None, ('brow', 'bcol')), may hold values from 0 to 31, as said below
- counts: int32 [16], P(('brow', 'bcol')), may hold values from 1 to 32, 320 in all
Outputs:
- hessian_blocks: float32 [16, 32, 256, 256], P(('brow', 'bcol'), 'token')
Inputs may be any that keep to these rules, and one draw needn't show every extreme that they name: `pairs`: reader r's pair rows lie in block rows 4 * (r // 2) to 4 * (r // 2) + 3, and each pair's row and column differ by less than 4.
All inputs are finite; a program needn't handle non-finite values. No bound on the sum of `counts` on one device may be relied on, other than what follows from the above.
Results may differ from a plain program's by a relative error of at most 0.0003.
Values may be sent and summed in bfloat16 or wider, within the bound.
A program may use at most 128 MiB of HBM per device.

v0:
```python
import jax
import jax.numpy as jnp
from jax import lax
from jax.sharding import PartitionSpec as P

BS = 256
BAND = 4


def extended(block, sides, width):
    for axis, dim in sides:
        count = lax.axis_size(axis)
        forward = [(i, i + 1) for i in range(count - 1)]
        backward = [(target, source) for source, target in forward]
        low = lax.ppermute(
            lax.slice_in_dim(block, block.shape[dim] - width, None, axis=dim), axis, forward
        )
        high = lax.ppermute(lax.slice_in_dim(block, 0, width, axis=dim), axis, backward)
        block = jnp.concatenate([low, block, high], axis=dim)
    return block


def shards(layer_input, pairs, counts):
    tok_rows = layer_input.shape[0]
    slot_total = pairs.shape[2]
    band_half = lax.all_gather(layer_input, "bcol", axis=1, tiled=True)
    band_width = band_half.shape[1]
    rim_width = (BAND - 1) * BS
    gathered = extended(band_half, (("brow", 1),), rim_width)
    block_rows = pairs[0, 0]
    block_cols = pairs[1, 0]
    live_count = counts[0]
    weight_factor = 2.0 / (tok_rows * lax.axis_size("token"))
    slot_ids_all = jnp.arange(slot_total, dtype=jnp.int32)
    keep_all = slot_ids_all < live_count
    own_rows = band_width // BS
    window_blocks = gathered.shape[1] // BS
    band_left = gathered[:, rim_width : rim_width + band_width]
    band_table = lax.dot_general(
        band_left, gathered, (((0,), (0,)), ((), ())), preferred_element_type=jnp.float32
    )
    band_table = band_table.reshape(own_rows, BS, window_blocks, BS)
    first_row = lax.axis_index("brow") * own_rows
    local_rows = block_rows - first_row
    local_cols = block_cols - first_row + BAND - 1
    picked = band_table[local_rows, :, local_cols, :] * weight_factor
    partial_sums = jnp.where(keep_all[:, None, None], picked, jnp.zeros_like(picked))
    summed = lax.psum_scatter(partial_sums, "token", scatter_dimension=0, tiled=True)
    return summed[None]


def solution(mesh):
    return jax.shard_map(
        shards,
        mesh=mesh,
        in_specs=(
            P("token", ("brow", "bcol")),
            P(None, ("brow", "bcol"), None),
            P(("brow", "bcol")),
        ),
        out_specs=P(("brow", "bcol"), "token", None, None),
        check_vma=False,
    )
```

profile of v0, /device:TPU:1, one launch (start us, length us, event | category | flops | bytes accessed | tf_op | source)
XLA Modules:
  0.0 230.1 jit_solution(4110361475086070654)
XLA Ops:
  6.5 0.0 copy-start.1
  6.5 0.0 all-gather.2.cloned.1.call-start
  6.5 0.7 all-gather.2.cloned.1.call-update
  7.3 0.0 reduce-scatter.2.cloned.1.call-start
  7.3 45.4 %all-gather.2.cloned.1.call-done = bf16[1024,1024]{1,0:T(8,128)(2,1)} async-done(((bf16[1024,512]{1,0:T(8,128)(2,1)}), bf16[1024,1024]{1,0:T(8,128)(2,1)}) %all-gather.2.cloned.1.call-update) | async-done | bytes 2097168 | tf_op jit(solution)/shard_map/all_gather | solution.py:26
  52.7 0.0 copy-start
  52.7 3.9 %fusion.11 = (bf16[1024,768]{1,0:T(8,128)(2,1)}, bf16[1024,768]{1,0:T(8,128)(2,1)}) fusion(bf16[1024,1024]{1,0:T(8,128)(2,1)} %all-gather.2.cloned.1.call-done), kind=kLoop, calls=%fused_computation.17 | loop fusion | bytes 6291456 | tf_op jit(solution)/shard_map/slice | solution.py:16
  56.6 4.4 %collective-permute-start = (bf16[1024,768]{1,0:T(8,128)(2,1)}, bf16[1024,768]{1,0:T(8,128)(2,1)}, u32[]{:S(2)}, u32[]{:S(2)}) collective-permute-start(bf16[1024,768]{1,0:T(8,128)(2,1)} %get-tuple-element.5), channel_id=1, source_target_pairs={{0,2},{2,4},{4,6},{6,8},{8,10},{10,12},{12,14},{1,3},{3,5},{5,7},{... | collective-permute-start | bytes 4718600 | tf_op jit(solution)/shard_map/ppermute | solution.py:15
  61.0 1.3 collective-permute-start.1
  62.9 0.0 copy-done.1
  63.0 30.2 %collective-permute-done = bf16[1024,768]{1,0:T(8,128)(2,1)} collective-permute-done((bf16[1024,768]{1,0:T(8,128)(2,1)}, bf16[1024,768]{1,0:T(8,128)(2,1)}, u32[]{:S(2)}, u32[]{:S(2)}) %collective-permute-start) | collective-permute-done | bytes 1572896 | tf_op jit(solution)/shard_map/ppermute | solution.py:15
  93.1 5.0 %collective-permute-done.1 = bf16[1024,768]{1,0:T(8,128)(2,1)} collective-permute-done((bf16[1024,768]{1,0:T(8,128)(2,1)}, bf16[1024,768]{1,0:T(8,128)(2,1)}, u32[]{:S(2)}, u32[]{:S(2)}) %collective-permute-start.1) | collective-permute-done | bytes 1572896 | tf_op jit(solution)/shard_map/ppermute | solution.py:18
  98.1 0.0 copy-done
  98.1 10.1 %convolution_bitcast_fusion = f32[1024,2560]{0,1:T(8,128)} fusion(bf16[1024,1024]{1,0:T(8,128)(2,1)S(1)} %copy-done, bf16[1024,768]{1,0:T(8,128)(2,1)} %collective-permute-done.1, bf16[1024,768]{1,0:T(8,128)(2,1)} %collective-permute-done), kind=kOutput, calls=%fused_computation.2 | convolution fusion | flops 5384437760 | bytes 15728640 | tf_op jit(solution)/shard_map/dot_general | solution.py:39
  108.2 13.0 %reshape.56 = f32[4,256,10,256]{1,0,3,2:T(4,128)} reshape(f32[1024,2560]{0,1:T(8,128)} %convolution_bitcast_fusion) | data formatting | bytes 20971520 | tf_op jit(solution)/shard_map/reshape | solution.py:42
  121.2 12.2 %copy.4 = f32[4,256,10,256]{3,1,2,0:T(8,128)} copy(f32[4,256,10,256]{1,0,3,2:T(4,128)} %reshape.56) | data formatting | bytes 20971520 | tf_op jit(solution)/shard_map/reshape | solution.py:42
  133.4 8.4 %gather_fusion = f32[32,256,256]{2,1,0:T(8,128)} fusion(f32[4,256,10,256]{3,1,2,0:T(8,128)} %copy.4, s32[32]{0:T(128)S(1)} %fusion.9), kind=kCustom, calls=%fused_computation | custom fusion | bytes 16777472 | tf_op jit(solution)/shard_map/gather | solution.py:46
  141.8 8.2 %multiply_select_fusion = f32[32,256,256]{2,1,0:T(8,128)} fusion(f32[32,256,256]{2,1,0:T(8,128)} %gather_fusion, pred[32]{0:T(512)(128)(4,1)S(1)} %iota_compare_fusion), kind=kLoop, calls=%fused_computation.1 | loop fusion | flops 4194304 | bytes 16777248 | tf_op jit(solution)/shard_map/jit(_where)/select_n | solution.py:47
  150.0 0.0 reduce-scatter.2.cloned.1.call-update
  150.1 73.2 %reduce-scatter.2.cloned.1.call-done = f32[2,256,256]{2,1,0:T(8,128)} async-done(((f32[32,256,256]{2,1,0:T(8,128)}), f32[2,256,256]{2,1,0:T(8,128)}) %reduce-scatter.2.cloned.1.call-update) | async-done | bytes 524304 | tf_op jit(solution)/shard_map/reduce_scatter | solution.py:48
  (2 shorter events, 0.0 us)
Async XLA Ops:
  6.5 56.4 %copy-start.1 = (s32[2,1,32]{2,1,0:T(1,128)S(1)}, s32[2,1,32]{2,1,0:T(1,128)}, u32[]{:S(2)}) copy-start(s32[2,1,32]{2,1,0:T(1,128)} %param.4) | copy-start | bytes 772
  6.5 46.2 %all-gather.2.cloned.1.call-start = ((), (), s32[]{:S(2)}) async-start(), calls=%async_computation.1 | async-start | bytes 3145728 | tf_op jit(solution)/shard_map/all_gather | solution.py:26
  7.3 216.0 %reduce-scatter.2.cloned.1.call-start = ((), (), s32[]{:S(2)}) async-start(), calls=%async_computation.2 | async-start | bytes 8912896 | tf_op jit(solution)/shard_map/reduce_scatter | solution.py:48
  52.7 45.4 %copy-start = (bf16[1024,1024]{1,0:T(8,128)(2,1)S(1)}, bf16[1024,1024]{1,0:T(8,128)(2,1)}, u32[]{:S(2)}) copy-start(bf16[1024,1024]{1,0:T(8,128)(2,1)} %all-gather.2.cloned.1.call-done) | copy-start | bytes 6291460
  56.6 36.5 %collective-permute-start = (bf16[1024,768]{1,0:T(8,128)(2,1)}, bf16[1024,768]{1,0:T(8,128)(2,1)}, u32[]{:S(2)}, u32[]{:S(2)}) collective-permute-start(bf16[1024,768]{1,0:T(8,128)(2,1)} %get-tuple-element.5), channel_id=1, source_target_pairs={{0,2},{2,4},{4,6},{6,8},{8,10},{10,12},{12,14},{1,3},{3,5},{5,7},{... | collective-permute-start | bytes 4718600 | tf_op jit(solution)/shard_map/ppermute | solution.py:15
  61.0 37.1 %collective-permute-start.1 = (bf16[1024,768]{1,0:T(8,128)(2,1)}, bf16[1024,768]{1,0:T(8,128)(2,1)}, u32[]{:S(2)}, u32[]{:S(2)}) collective-permute-start(bf16[1024,768]{1,0:T(8,128)(2,1)} %get-tuple-element.6), channel_id=1, source_target_pairs={{2,0},{4,2},{6,4},{8,6},{10,8},{12,10},{14,12},{3,1},{5,3},{7,5},{... | collective-permute-start | bytes 4718600 | tf_op jit(solution)/shard_map/ppermute | solution.py:18
Sparse Core Ops, SparseCore 0:
  9.2 43.4 all-gather.1
  150.2 73.0 reduce-scatter.1
where the time goes:
time: 233 us; the launch traced here: 230 us
  waiting for transfers between devices  154 us (66%)
  local copies, waits for them, and re-layouts  37.5 us (16%)
  between operations  14.1 us (6%)
  matrix products  10.1 us (4%)
  other arithmetic  8.21 us (4%)
  starting transfers between devices  5.71 us (2%)
    reduce_scatter x1, waiting for transfers between devices, shards(): lax.psum_scatter(partial_sums, 'token', scatter_dimension=0, tiled=True)  73.2 us
    all_gather x1, waiting for transfers between devices, shards(): band_half = lax.all_gather(layer_input, 'bcol', axis=1, tiled=True)  45.4 us
    ppermute x1, waiting for transfers between devices, extended(): lax.ppermute(lax.slice_in_dim(block, block.shape[dim] - width, None, axis...  30.2 us
    reshape x2, local copies, waits for them, and re-layouts, shards(): band_table = band_table.reshape(own_rows, BS, window_blocks, BS)  25.2 us
    dot_general x1, matrix products, shards(): lax.dot_general(band_left, gathered, (((0,), (0,)), ((), ())), preferred_...  10.1 us
    gather x1, local copies, waits for them, and re-layouts, shards(): picked = band_table[local_rows, :, local_cols, :] * weight_factor  8.41 us
    select_n x1, other arithmetic, shards(): jnp.where(keep_all[:, None, None], picked, jnp.zeros_like(picked))  8.19 us
    ppermute x1, waiting for transfers between devices, extended(): lax.ppermute(lax.slice_in_dim(block, 0, width, axis=dim), axis, backward)  4.99 us
  transfers between devices with their start and end apart: 4, of which 4 were waited for; matrix products, arithmetic and copies ran while one was open for 0% of the time, Pallas kernels for 0%

commit v1 on v0

v1 whole, which is shorter than its diff:
```python
import functools
import jax
import jax.numpy as jnp
from jax import lax
from jax.experimental import pallas as pl
from jax.experimental.pallas import tpu as pltpu
from jax.sharding import PartitionSpec as P

BS = 256
BAND = 4
NX, NY, NZ = 4, 4, 8
CHIPS = NX * NY
CHUNKS = 4
MESH = pl.DeviceIdType.MESH

TABLE = {
    (0, 0): (0, 0), (0, 1): (1, 0), (1, 1): (2, 0),
    (2, 2): (3, 0), (2, 3): (4, 0), (3, 3): (5, 0),
    (1, 4): (6, 0), (3, 6): (7, 0),
    (0, 2): (8, 0), (0, 3): (9, 0), (1, 2): (10, 0), (1, 3): (11, 0),
    (0, -2): (12, 0), (0, -1): (13, 0), (1, -2): (14, 0), (1, -1): (15, 0),
    (2, 4): (16, 1), (3, 4): (17, 1), (2, 5): (18, 1), (3, 5): (19, 1),
    (0, -3): (20, 1), (2, -1): (21, 1),
    (1, 0): (1, 1), (3, 2): (4, 1),
    (2, 0): (8, 1), (3, 0): (9, 1), (2, 1): (10, 1), (3, 1): (11, 1),
}
WIDTH = 2 * BAND - 1


def device(x, y, z, k):
    return (((x % 2) * NY + y) * 2 + k, z, x // 2)


def gram(a, b):
    return lax.dot_general(a, b, (((0,), (0,)), ((), ())), preferred_element_type=jnp.float32)


def kernel(
    weight, x_ref, pairs_ref, counts_ref, out_ref,
    own, cross, below, ahead, p_own, p_mid, p_low, k_own, k_mid, k_low,
    r_own, r_mid, r_low, table, stage, arrived, pairs_far, pairs_all, lookup,
    local_sem, x_send, x_recv, zf_send, zf_recv, ze_send, ze_recv, pr_send, pr_recv,
    core_send, core_recv, rs_send, rs_recv, hop_send, hop_recv, out_send, out_recv,
):
    token = lax.axis_index("token")
    z = lax.axis_index("brow")
    c = lax.axis_index("bcol")
    k = token % 2
    y = (token // 2) % NY
    x = 2 * c + token // (2 * NY)
    me = y * NX + x
    half = x_ref.shape[0] // 2
    step = half // CHUNKS
    up, down = (z + 1) % NZ, (z + NZ - 1) % NZ

    load = pltpu.make_async_copy(x_ref, own, local_sem.at[0])
    load.start()
    load_pairs = pltpu.make_async_copy(pairs_ref, pairs_all.at[c], local_sem.at[1])
    load_pairs.start()

    barrier = pltpu.get_barrier_semaphore()

    def plane_peer(o):
        return (x + o % NX) % NX, (y + (o // NX) % NY) % NY, (k + o // CHIPS) % 2

    def greet(o, carry):
        px, py, pk = plane_peer(o)
        pl.semaphore_signal(barrier, inc=1, device_id=device(px, py, z, pk), device_id_type=MESH)
        return carry

    lax.fori_loop(1, 2 * CHIPS, greet, 0)
    pl.semaphore_signal(barrier, inc=1, device_id=device(x, y, up, k), device_id_type=MESH)
    pl.semaphore_signal(barrier, inc=1, device_id=device(x, y, down, k), device_id_type=MESH)
    for (row, col), (at, flip) in TABLE.items():
        lookup[row * WIDTH + col - row + BAND - 1] = at * 2 + flip
    pl.semaphore_wait(barrier, 2 * CHIPS + 1)

    def x_copy(direction, j):
        to = device((x + 1) % NX, y, z, k) if direction == 0 else device((x + NX - 1) % NX, y, z, k)
        first = (c if direction == 0 else 1 - c) * half + j * step
        return pltpu.make_async_remote_copy(
            src_ref=x_ref.at[pl.ds(first, step), :],
            dst_ref=cross.at[c, pl.ds(j * step, step), :],
            send_sem=x_send.at[direction, j],
            recv_sem=x_recv.at[c, j],
            device_id=to, device_id_type=MESH,
        )

    def x_arrival(side, j):
        return pltpu.make_async_remote_copy(
            src_ref=x_ref.at[pl.ds(0, step), :],
            dst_ref=cross.at[side, pl.ds(j * step, step), :],
            send_sem=x_send.at[0, j],
            recv_sem=x_recv.at[side, j],
            device_id=device((x + 1) % NX, y, z, k), device_id_type=MESH,
        )

    def forward(j):
        return pltpu.make_async_remote_copy(
            src_ref=cross.at[1, pl.ds(j * step, step), :],
            dst_ref=below.at[pl.ds(j * step, step), :],
            send_sem=zf_send.at[j], recv_sem=zf_recv.at[j],
            device_id=device(x, y, up, k), device_id_type=MESH,
        )

    for j in range(CHUNKS):
        x_copy(0, j).start()
        x_copy(1, j).start()
    edge = pltpu.make_async_remote_copy(
        src_ref=x_ref.at[:, pl.ds(0, BS)], dst_ref=ahead,
        send_sem=ze_send, recv_sem=ze_recv,
        device_id=device(x, y, down, k), device_id_type=MESH,
    )
    edge.start()
    share_pairs = pltpu.make_async_remote_copy(
        src_ref=pairs_ref, dst_ref=pairs_far, send_sem=pr_send, recv_sem=pr_recv,
        device_id=device((x + 2) % NX, y, z, k), device_id_type=MESH,
    )
    share_pairs.start()

    def put(ref, q, value):
        ref[:, :, :, q * 8 : q * 8 + 8, :] = value.reshape(2, NY, NX, 8, BS)

    def to_sibling(g, part, got):
        return pltpu.make_async_remote_copy(
            src_ref=part.at[1 - k], dst_ref=got,
            send_sem=core_send.at[g], recv_sem=core_recv.at[g],
            device_id=device(x, y, z, 1 - k), device_id_type=MESH,
        )

    def scatter_copy(g, got, land, o):
        px, py = (x + o % NX) % NX, (y + o // NX) % NY
        return pltpu.make_async_remote_copy(
            src_ref=got.at[py, px], dst_ref=land.at[me],
            send_sem=rs_send.at[g, o], recv_sem=rs_recv.at[g, me],
            device_id=device(px, py, z, k), device_id_type=MESH,
        )

    def scatter_arrival(g, got, land, o):
        px, py = (x + o % NX) % NX, (y + o // NX) % NY
        source = py * NX + px
        return pltpu.make_async_remote_copy(
            src_ref=got.at[py, px], dst_ref=land.at[source],
            send_sem=rs_send.at[g, o], recv_sem=rs_recv.at[g, source],
            device_id=device(px, py, z, k), device_id_type=MESH,
        )

    def scatter(g, part, got, land):
        copy = to_sibling(g, part, got)
        copy.wait()
        for row in range(NY):
            got[row] = got[row] + part[k, row]

        def send(o, carry):
            scatter_copy(g, got, land, o).start()
            return carry

        lax.fori_loop(1, CHIPS, send, 0)
        land[me] = got[y, x]

    def collect(g, got, land):
        def take(o, carry):
            scatter_arrival(g, got, land, o).wait_recv()
            return carry

        lax.fori_loop(1, CHIPS, take, 0)

    load.wait()
    put(p_own, 0, gram(own[:, :BS], own[:, :BS]))
    put(p_own, 1, gram(own[:, :BS], own[:, BS:]))
    put(p_own, 2, gram(own[:, BS:], own[:, BS:]))
    to_sibling(0, p_own, k_own).start()

    for j in range(CHUNKS):
        x_arrival(1, j).wait_recv()
        forward(j).start()
    scatter(0, p_own, k_own, r_own)
    for j in range(CHUNKS):
        x_arrival(0, j).wait_recv()

    for i in range(2):
        for j in range(2):
            put(p_mid, 1 + 2 * i + j, gram(cross[0, :, i * BS : (i + 1) * BS], cross[1, :, j * BS : (j + 1) * BS]))
    edge.wait_recv()
    put(p_mid, 0, gram(own[:, BS:], ahead[...]))
    to_sibling(1, p_mid, k_mid).start()
    scatter(1, p_mid, k_mid, r_mid)

    for j in range(CHUNKS):
        forward(j).wait_recv()
    for i in range(2):
        for j in range(2):
            put(p_low, 2 * i + j, gram(cross[0, :, i * BS : (i + 1) * BS], below[:, j * BS : (j + 1) * BS]))
    to_sibling(2, p_low, k_low).start()
    scatter(2, p_low, k_low, r_low)

    share_pairs.wait_recv()
    load_pairs.wait()
    far = pltpu.make_async_copy(pairs_far, pairs_all.at[1 - c], local_sem.at[2])
    far.start()

    collect(0, k_own, r_own)
    for side in range(2):
        total = None
        for row in range(NY):
            for col in range(2):
                term = r_own[row * NX + 2 * side + col]
                total = term if total is None else total + term
        table[3 * side : 3 * side + 3] = total.reshape(3, 8, BS)
    collect(1, k_mid, r_mid)
    for side in range(2):
        total = None
        for row in range(NY):
            for col in range(2):
                term = r_mid[row * NX + 2 * side + col, 0:8, :]
                total = term if total is None else total + term
        table[6 + side] = total
    hop_up = pltpu.make_async_remote_copy(
        src_ref=table.at[pl.ds(6, 2)], dst_ref=table.at[pl.ds(20, 2)],
        send_sem=hop_send.at[0], recv_sem=hop_recv.at[0],
        device_id=device(x, y, up, k), device_id_type=MESH,
    )
    hop_up.start()
    total = r_mid[0, 8:40, :]
    for source in range(1, CHIPS):
        total = total + r_mid[source, 8:40, :]
    table[8:12] = total.reshape(4, 8, BS)
    collect(2, k_low, r_low)
    total = r_low[0]
    for source in range(1, CHIPS):
        total = total + r_low[source]
    table[12:16] = total.reshape(4, 8, BS)
    hop_down = pltpu.make_async_remote_copy(
        src_ref=table.at[pl.ds(12, 4)], dst_ref=table.at[pl.ds(16, 4)],
        send_sem=hop_send.at[1], recv_sem=hop_recv.at[1],
        device_id=device(x, y, down, k), device_id_type=MESH,
    )
    hop_down.start()
    far.wait()
    hop_up.wait()
    hop_down.wait()

    def code(reader, slot):
        row = pairs_all[reader, 0, 0, slot]
        col = pairs_all[reader, 1, 0, slot]
        at = (row - z * BAND) * WIDTH + col - row + BAND - 1
        return lookup[jnp.clip(at, 0, BAND * WIDTH - 1)]

    def fill(o, px, py, pk):
        slot = 2 * (((px % 2) * NY + py) * 2 + pk)
        reader = px // 2
        stage[o, 0] = table[code(reader, slot) // 2]
        stage[o, 1] = table[code(reader, slot + 1) // 2]

    rank = k * CHIPS + me

    def deliver(o):
        px, py, pk = plane_peer(o)
        return pltpu.make_async_remote_copy(
            src_ref=stage.at[o], dst_ref=arrived.at[rank],
            send_sem=out_send.at[o], recv_sem=out_recv.at[rank],
            device_id=device(px, py, z, pk), device_id_type=MESH,
        )

    def send_out(o, carry):
        px, py, pk = plane_peer(o)
        fill(o, px, py, pk)
        deliver(o).start()
        return carry

    lax.fori_loop(1, 2 * CHIPS, send_out, 0)
    fill(0, x, y, k)
    arrived[rank] = stage[0]

    def take_out(o, carry):
        px, py, pk = plane_peer(o)
        source = pk * CHIPS + py * NX + px
        pltpu.make_async_remote_copy(
            src_ref=stage.at[o], dst_ref=arrived.at[source],
            send_sem=out_send.at[o], recv_sem=out_recv.at[source],
            device_id=device(px, py, z, pk), device_id_type=MESH,
        ).wait_recv()
        return carry

    lax.fori_loop(1, 2 * CHIPS, take_out, 0)
    for s in range(2):
        slot = 2 * token + s
        block = arrived[:, s].reshape(BS, BS)
        flip = code(c, slot) % 2 == 1
        block = jnp.where(flip, block.T, block)
        out_ref[0, s] = jnp.where(slot < counts_ref[0], block * weight, 0.0)

    for j in range(CHUNKS):
        x_copy(0, j).wait_send()
        x_copy(1, j).wait_send()
        forward(j).wait_send()
    edge.wait_send()
    share_pairs.wait_send()
    for g, (got, land) in enumerate(((k_own, r_own), (k_mid, r_mid), (k_low, r_low))):
        def left(o, carry):
            scatter_copy(g, got, land, o).wait_send()
            return carry

        lax.fori_loop(1, CHIPS, left, 0)

    def left_out(o, carry):
        deliver(o).wait_send()
        return carry

    lax.fori_loop(1, 2 * CHIPS, left_out, 0)


def shards(layer_input, pairs, counts):
    rows, columns = layer_input.shape
    weight = 2.0 / (rows * lax.axis_size("token"))
    dma, vmem = pltpu.SemaphoreType.DMA, pltpu.VMEM
    f32, bf16 = jnp.float32, jnp.bfloat16
    slots = pairs.shape[2] // lax.axis_size("token")
    scratch = [
        vmem((rows, columns), bf16),
        vmem((2, rows // 2, columns), bf16),
        vmem((rows // 2, columns), bf16),
        vmem((rows, BS), bf16),
    ]
    heights = (24, 40, 32)
    scratch += [vmem((2, NY, NX, h, BS), f32) for h in heights]
    scratch += [vmem((NY, NX, h, BS), f32) for h in heights]
    scratch += [vmem((CHIPS, h, BS), f32) for h in heights]
    scratch += [
        vmem((22, 8, BS), f32),
        vmem((2 * CHIPS, slots, 8, BS), f32),
        vmem((2 * CHIPS, slots, 8, BS), f32),
        vmem(pairs.shape, jnp.int32),
        pltpu.SMEM((2,) + pairs.shape, jnp.int32),
        pltpu.SMEM((BAND * WIDTH,), jnp.int32),
        dma((3,)),
        dma((2, CHUNKS)), dma((2, CHUNKS)),
        dma((CHUNKS,)), dma((CHUNKS,)),
        dma, dma, dma, dma,
        dma((3,)), dma((3,)),
        dma((3, CHIPS)), dma((3, CHIPS)),
        dma((2,)), dma((2,)),
        dma((2 * CHIPS,)), dma((2 * CHIPS,)),
    ]
    return pl.pallas_call(
        functools.partial(kernel, weight),
        out_shape=jax.ShapeDtypeStruct((1, slots, BS, BS), f32),
        in_specs=[
            pl.BlockSpec(memory_space=pl.ANY),
            pl.BlockSpec(memory_space=pl.ANY),
            pl.BlockSpec(memory_space=pltpu.SMEM),
        ],
        out_specs=pl.BlockSpec(memory_space=pltpu.VMEM),
        scratch_shapes=scratch,
        compiler_params=pltpu.CompilerParams(
            collective_id=0, has_side_effects=True, vmem_limit_bytes=48 * 2**20
        ),
    )(layer_input, pairs, counts)


def solution(mesh):
    return jax.shard_map(
        shards,
        mesh=mesh,
        in_specs=(
            P("token", ("brow", "bcol")),
            P(None, ("brow", "bcol"), None),
            P(("brow", "bcol")),
        ),
        out_specs=P(("brow", "bcol"), "token", None, None),
        check_vma=False,
    )
```

time: 233 us -> 59.6 us (0.26); the launches traced: 230 us -> 59.5 us
  waiting for transfers between devices: 154 us -> 0 us
  Pallas kernels: 0 us -> 56.8 us
  local copies, waits for them, and re-layouts: 37.5 us -> 2.03 us
  between operations: 14.1 us -> 0.68 us
  matrix products: 10.1 us -> 0 us
  other arithmetic: 8.21 us -> 0 us
  starting transfers between devices: 5.71 us -> 0 us
    reduce_scatter x1 -> x0, waiting for transfers between devices: 73.2 us -> none  [shards(): lax.psum_scatter(partial_sums, 'token', scatter_dimension=0, tiled=True)]
    pallas_call x0 -> x1, Pallas kernels: none -> 56.8 us  [shards(): pl.pallas_call(functools.partial(kernel, weight), out_shape=jax.ShapeDtyp...]
    all_gather x1 -> x0, waiting for transfers between devices: 45.4 us -> none  [shards(): band_half = lax.all_gather(layer_input, 'bcol', axis=1, tiled=True)]
    ppermute x2 -> x0, waiting for transfers between devices: 35.2 us -> none  [the longest x1 30.2 us: extended(): lax.ppermute(lax.slice_in_dim(block, block.shape[dim] - width, None, axis...]
    reshape x2 -> x0, local copies, waits for them, and re-layouts: 25.2 us -> none  [shards(): band_table = band_table.reshape(own_rows, BS, window_blocks, BS)]
    dot_general x1 -> x0, matrix products: 10.1 us -> none  [shards(): lax.dot_general(band_left, gathered, (((0,), (0,)), ((), ())), preferred_...]
    gather x1 -> x0, local copies, waits for them, and re-layouts: 8.41 us -> none  [shards(): picked = band_table[local_rows, :, local_cols, :] * weight_factor]
    select_n x1 -> x0, other arithmetic: 8.19 us -> none  [shards(): jnp.where(keep_all[:, None, None], picked, jnp.zeros_like(picked))]
  transfers between devices with their start and end apart: 4 -> 0, of which waited for: 4 -> 0; matrix products, arithmetic and copies ran while one was open for 0% -> 0% of each run, Pallas kernels for 0% -> 0%
where the time goes in v1:
time: 59.6 us; the launch traced here: 59.5 us
  Pallas kernels  56.8 us (95%)
  local copies, waits for them, and re-layouts  2.03 us (3%)
  between operations  0.68 us (1%)
    pallas_call x1, Pallas kernels, shards(): pl.pallas_call(functools.partial(kernel, weight), out_shape=jax.ShapeDtyp...  56.8 us
    unnamed x5, local copies, waits for them, and re-layouts  2.03 us

profile of v1, /device:TPU:1, one launch (start us, length us, event | category | flops | bytes accessed | tf_op | source)
XLA Modules:
  0.0 59.5 jit_solution(12425807211684129769)
XLA Ops:
  0.0 0.0 copy-start.1
  0.7 0.0 copy-done.1
  0.7 0.0 copy-start
  0.7 1.2 %copy-done = bf16[1024,512]{1,0:T(8,128)(2,1)S(1)} copy-done((bf16[1024,512]{1,0:T(8,128)(2,1)S(1)}, bf16[1024,512]{1,0:T(8,128)(2,1)}, u32[]{:S(2)}) %copy-start) | copy-done | bytes 1048600
  1.9 56.8 %shard_map.37 = f32[1,2,256,256]{3,2,1,0:T(8,128)S(1)} custom-call(bf16[1024,512]{1,0:T(8,128)(2,1)S(1)} %copy-done, s32[2,1,32]{2,1,0:T(1,128)S(1)} %copy-done.1, s32[1]{0:T(128)S(6)} %copy.5.counts_ref), custom_call_target="tpu_custom_call" | custom-call | tf_op jit(solution)/shard_map/pallas_call | solution.py:345
  58.7 0.8 %copy.6 = f32[1,2,256,256]{3,2,1,0:T(8,128)} copy(f32[1,2,256,256]{3,2,1,0:T(8,128)S(1)} %shard_map.37) | data formatting | bytes 1048576
Async XLA Ops:
  0.0 0.7 %copy-start.1 = (s32[2,1,32]{2,1,0:T(1,128)S(1)}, s32[2,1,32]{2,1,0:T(1,128)}, u32[]{:S(2)}) copy-start(s32[2,1,32]{2,1,0:T(1,128)} %pairs_ref.1) | copy-start | bytes 772
  0.7 1.2 %copy-start = (bf16[1024,512]{1,0:T(8,128)(2,1)S(1)}, bf16[1024,512]{1,0:T(8,128)(2,1)}, u32[]{:S(2)}) copy-start(bf16[1024,512]{1,0:T(8,128)(2,1)} %x_ref.1) | copy-start | bytes 3145732

commit v2 on v1

--- a/solution.py
+++ b/solution.py
@@ -10,7 +10,8 @@
 BAND = 4
 NX, NY, NZ = 4, 4, 8
 CHIPS = NX * NY
-CHUNKS = 4
+CHUNKS = 8
+WINDOW = 3
 MESH = pl.DeviceIdType.MESH
 
 TABLE = {
@@ -40,7 +41,7 @@
     own, cross, below, ahead, p_own, p_mid, p_low, k_own, k_mid, k_low,
     r_own, r_mid, r_low, table, stage, arrived, pairs_far, pairs_all, lookup,
     local_sem, x_send, x_recv, zf_send, zf_recv, ze_send, ze_recv, pr_send, pr_recv,
-    core_send, core_recv, rs_send, rs_recv, hop_send, hop_recv, out_send, out_recv,
+    core_send, core_recv, y_own, s_own, y_send, y_recv, row_send, row_recv, rs_send, rs_recv, hop_send, hop_recv, out_send, out_recv,
 ):
     token = lax.axis_index("token")
     z = lax.axis_index("brow")
@@ -63,17 +64,14 @@
     def plane_peer(o):
         return (x + o % NX) % NX, (y + (o // NX) % NY) % NY, (k + o // CHIPS) % 2
 
-    def greet(o, carry):
-        px, py, pk = plane_peer(o)
-        pl.semaphore_signal(barrier, inc=1, device_id=device(px, py, z, pk), device_id_type=MESH)
-        return carry
-
-    lax.fori_loop(1, 2 * CHIPS, greet, 0)
-    pl.semaphore_signal(barrier, inc=1, device_id=device(x, y, up, k), device_id_type=MESH)
-    pl.semaphore_signal(barrier, inc=1, device_id=device(x, y, down, k), device_id_type=MESH)
+    near = [device((x + o) % NX, y, z, k) for o in (2, 1, 3)]
+    near += [device(x, (y + o) % NY, z, k) for o in (2, 1, 3)]
+    near += [device(x, y, up, k), device(x, y, down, k), device(x, y, z, 1 - k)]
+    for peer in near:
+        pl.semaphore_signal(barrier, inc=1, device_id=peer, device_id_type=MESH)
     for (row, col), (at, flip) in TABLE.items():
         lookup[row * WIDTH + col - row + BAND - 1] = at * 2 + flip
-    pl.semaphore_wait(barrier, 2 * CHIPS + 1)
+    pl.semaphore_wait(barrier, len(near))
 
     def x_copy(direction, j):
         to = device((x + 1) % NX, y, z, k) if direction == 0 else device((x + NX - 1) % NX, y, z, k)
@@ -103,7 +101,7 @@
             device_id=device(x, y, up, k), device_id_type=MESH,
         )
 
-    for j in range(CHUNKS):
+    for j in range(WINDOW):
         x_copy(0, j).start()
         x_copy(1, j).start()
     edge = pltpu.make_async_remote_copy(
@@ -165,6 +163,36 @@
 
         lax.fori_loop(1, CHIPS, take, 0)
 
+    def y_copy(o, source):
+        return pltpu.make_async_remote_copy(
+            src_ref=k_own.at[(y + o) % NY], dst_ref=y_own.at[source],
+            send_sem=y_send.at[o], recv_sem=y_recv.at[source],
+            device_id=device(x, (y + o) % NY, z, k), device_id_type=MESH,
+        )
+
+    def row_copy(o, source):
+        return pltpu.make_async_remote_copy(
+            src_ref=s_own.at[(x + o) % NX], dst_ref=r_own.at[source],
+            send_sem=row_send.at[o], recv_sem=row_recv.at[source],
+            device_id=device((x + o) % NX, y, z, k), device_id_type=MESH,
+        )
+
+    def own_along_y():
+        to_sibling(0, p_own, k_own).wait()
+        for row in range(NY):
+            k_own[row] = k_own[row] + p_own[k, row]
+        for o in range(1, NY):
+            y_copy(o, y).start()
+        y_own[y] = k_own[y]
+
+    def own_along_x():
+        for o in range(1, NY):
+            y_copy(o, (y + o) % NY).wait_recv()
+        s_own[...] = (y_own[0] + y_own[1]) + (y_own[2] + y_own[3])
+        for o in range(1, NX):
+            row_copy(o, x).start()
+        r_own[x] = s_own[x]
+
     load.wait()
     put(p_own, 0, gram(own[:, :BS], own[:, :BS]))
     put(p_own, 1, gram(own[:, :BS], own[:, BS:]))
@@ -174,9 +202,21 @@
     for j in range(CHUNKS):
         x_arrival(1, j).wait_recv()
         forward(j).start()
-    scatter(0, p_own, k_own, r_own)
+        x_copy(0, j).wait_send()
+        x_copy(1, j).wait_send()
+        if j + WINDOW < CHUNKS:
+            x_copy(0, j + WINDOW).start()
+            x_copy(1, j + WINDOW).start()
+        if j == 0:
+            own_along_y()
+        if j == CHUNKS - 3:
+            own_along_x()
     for j in range(CHUNKS):
         x_arrival(0, j).wait_recv()
+    share_pairs.wait_recv()
+    load_pairs.wait()
+    far = pltpu.make_async_copy(pairs_far, pairs_all.at[1 - c], local_sem.at[2])
+    far.start()
 
     for i in range(2):
         for j in range(2):
@@ -194,19 +234,10 @@
     to_sibling(2, p_low, k_low).start()
     scatter(2, p_low, k_low, r_low)
 
-    share_pairs.wait_recv()
-    load_pairs.wait()
-    far = pltpu.make_async_copy(pairs_far, pairs_all.at[1 - c], local_sem.at[2])
-    far.start()
-
-    collect(0, k_own, r_own)
+    for o in range(1, NX):
+        row_copy(o, (x + o) % NX).wait_recv()
     for side in range(2):
-        total = None
-        for row in range(NY):
-            for col in range(2):
-                term = r_own[row * NX + 2 * side + col]
-                total = term if total is None else total + term
-        table[3 * side : 3 * side + 3] = total.reshape(3, 8, BS)
+        table[3 * side : 3 * side + 3] = (r_own[2 * side] + r_own[2 * side + 1]).reshape(3, 8, BS)
     collect(1, k_mid, r_mid)
     for side in range(2):
         total = None
@@ -291,12 +322,14 @@
         out_ref[0, s] = jnp.where(slot < counts_ref[0], block * weight, 0.0)
 
     for j in range(CHUNKS):
-        x_copy(0, j).wait_send()
-        x_copy(1, j).wait_send()
         forward(j).wait_send()
+    for o in range(1, NY):
+        y_copy(o, y).wait_send()
+    for o in range(1, NX):
+        row_copy(o, x).wait_send()
     edge.wait_send()
     share_pairs.wait_send()
-    for g, (got, land) in enumerate(((k_own, r_own), (k_mid, r_mid), (k_low, r_low))):
+    for g, got, land in ((1, k_mid, r_mid), (2, k_low, r_low)):
         def left(o, carry):
             scatter_copy(g, got, land, o).wait_send()
             return carry
@@ -325,7 +358,7 @@
     heights = (24, 40, 32)
     scratch += [vmem((2, NY, NX, h, BS), f32) for h in heights]
     scratch += [vmem((NY, NX, h, BS), f32) for h in heights]
-    scratch += [vmem((CHIPS, h, BS), f32) for h in heights]
+    scratch += [vmem((n, h, BS), f32) for n, h in zip((NX, CHIPS, CHIPS), heights)]
     scratch += [
         vmem((22, 8, BS), f32),
         vmem((2 * CHIPS, slots, 8, BS), f32),
@@ -338,6 +371,8 @@
         dma((CHUNKS,)), dma((CHUNKS,)),
         dma, dma, dma, dma,
         dma((3,)), dma((3,)),
+        vmem((NY, NX, heights[0], BS), f32), vmem((NX, heights[0], BS), f32),
+        dma((NY,)), dma((NY,)), dma((NX,)), dma((NX,)),
         dma((3, CHIPS)), dma((3, CHIPS)),
         dma((2,)), dma((2,)),
         dma((2 * CHIPS,)), dma((2 * CHIPS,)),
@@ -346,14 +381,14 @@
         functools.partial(kernel, weight),
         out_shape=jax.ShapeDtypeStruct((1, slots, BS, BS), f32),
         in_specs=[
-            pl.BlockSpec(memory_space=pl.ANY),
-            pl.BlockSpec(memory_space=pl.ANY),
+            pl.BlockSpec(memory_space=pltpu.HBM),
+            pl.BlockSpec(memory_space=pltpu.HBM),
             pl.BlockSpec(memory_space=pltpu.SMEM),
         ],
         out_specs=pl.BlockSpec(memory_space=pltpu.VMEM),
         scratch_shapes=scratch,
         compiler_params=pltpu.CompilerParams(
-            collective_id=0, has_side_effects=True, vmem_limit_bytes=48 * 2**20
+            collective_id=0, has_side_effects=True, vmem_limit_bytes=62 * 2**20
         ),
     )(layer_input, pairs, counts)
 

time: 59.6 us -> 59.2 us (level)
    unnamed x5 -> x1, local copies, waits for them, and re-layouts: 2.03 us -> 1.87 us
where the time goes in v2:
time: 59.2 us; the launch traced here: 59 us
  Pallas kernels  56.5 us (95%)
  local copies, waits for them, and re-layouts  1.87 us (3%)
  between operations  0.66 us (1%)
    pallas_call x1, Pallas kernels, shards(): pl.pallas_call(functools.partial(kernel, weight), out_shape=jax.ShapeDtyp...  56.5 us
    unnamed x1, local copies, waits for them, and re-layouts  1.87 us

profile of v2, /device:TPU:1, one launch (start us, length us, event | category | flops | bytes accessed | tf_op | source)
XLA Modules:
  0.0 59.0 jit_solution(16493273631712756212)
XLA Ops:
  0.7 56.5 %shard_map.37 = f32[1,2,256,256]{3,2,1,0:T(8,128)} custom-call(bf16[1024,512]{1,0:T(8,128)(2,1)} %x_ref.1, s32[2,1,32]{2,1,0:T(1,128)} %pairs_ref.1, s32[1]{0:T(128)S(6)} %copy.5.counts_ref), custom_call_target="tpu_custom_call" | custom-call | tf_op jit(solution)/shard_map/pallas_call | solution.py:380
  57.2 1.9 %copy.6 = f32[1,2,256,256]{3,2,1,0:T(8,128)} copy(f32[1,2,256,256]{3,2,1,0:T(8,128)} %shard_map.37) | data formatting | bytes 1048576

commit v3 on v2

--- a/solution.py
+++ b/solution.py
@@ -11,7 +11,7 @@
 NX, NY, NZ = 4, 4, 8
 CHIPS = NX * NY
 CHUNKS = 8
-WINDOW = 3
+PARTS = 4
 MESH = pl.DeviceIdType.MESH
 
 TABLE = {
@@ -38,10 +38,10 @@
 
 def kernel(
     weight, x_ref, pairs_ref, counts_ref, out_ref,
-    own, cross, below, ahead, p_own, p_mid, p_low, k_own, k_mid, k_low,
-    r_own, r_mid, r_low, table, stage, arrived, pairs_far, pairs_all, lookup,
+    own, cross, below, ahead, far_rows, far_cols, far_below, far_own, far_ahead,
+    p_own, k_own, p_mid, p_low, r_own, r_mid, r_low, table, stage, arrived, pairs_far, pairs_all, lookup,
     local_sem, x_send, x_recv, zf_send, zf_recv, ze_send, ze_recv, pr_send, pr_recv,
-    core_send, core_recv, y_own, s_own, y_send, y_recv, row_send, row_recv, rs_send, rs_recv, hop_send, hop_recv, out_send, out_recv,
+    core_send, core_recv, swap_send, swap_recv, y_own, s_own, y_send, y_recv, row_send, row_recv, rs_send, rs_recv, hop_send, hop_recv, out_send, out_recv,
 ):
     token = lax.axis_index("token")
     z = lax.axis_index("brow")
@@ -101,7 +101,7 @@
             device_id=device(x, y, up, k), device_id_type=MESH,
         )
 
-    for j in range(WINDOW):
+    for j in range(CHUNKS):
         x_copy(0, j).start()
         x_copy(1, j).start()
     edge = pltpu.make_async_remote_copy(
@@ -116,13 +116,45 @@
     )
     share_pairs.start()
 
+    def swap(n, source, target):
+        return pltpu.make_async_remote_copy(
+            src_ref=source, dst_ref=target,
+            send_sem=swap_send.at[n], recv_sem=swap_recv.at[n],
+            device_id=device(x, y, z, 1 - k), device_id_type=MESH,
+        )
+
+    def strip(ref, block, core, *lead):
+        first = pl.multiple_of(block * BS + core * (BS // 2), BS // 2)
+        return ref.at[lead + (slice(None), pl.ds(first, BS // 2))]
+
+    part = half // PARTS
+
+    def swap_rows(g, i):
+        rows = pl.ds(g * part, part)
+        first = pl.multiple_of(i * BS + (1 - k) * (BS // 2), BS // 2)
+        return swap(
+            2 * g + i, cross.at[0, rows, pl.ds(first, BS // 2)],
+            far_rows.at[rows, i * (BS // 2) : (i + 1) * (BS // 2)],
+        )
+
+    def swap_cols(g):
+        rows = pl.ds(g * part, part)
+        return swap(2 * PARTS + g, cross.at[1, rows, :], far_cols.at[rows, :])
+
+    def swap_below(g):
+        rows = pl.ds(g * part, part)
+        return swap(3 * PARTS + g, below.at[rows, :], far_below.at[rows, :])
+
+    swap_own = swap(4 * PARTS, strip(own, 1, 1 - k), far_own)
+    swap_ahead = swap(4 * PARTS + 1, ahead, far_ahead)
+
     def put(ref, q, value):
-        ref[:, :, :, q * 8 : q * 8 + 8, :] = value.reshape(2, NY, NX, 8, BS)
-
-    def to_sibling(g, part, got):
-        return pltpu.make_async_remote_copy(
-            src_ref=part.at[1 - k], dst_ref=got,
-            send_sem=core_send.at[g], recv_sem=core_recv.at[g],
+        ref[..., q * 8 : q * 8 + 8, :] = value.reshape(ref.shape[:-2] + (8, BS))
+
+    def to_sibling():
+        return pltpu.make_async_remote_copy(
+            src_ref=p_own.at[1 - k], dst_ref=k_own,
+            send_sem=core_send, recv_sem=core_recv,
             device_id=device(x, y, z, 1 - k), device_id_type=MESH,
         )
 
@@ -143,12 +175,7 @@
             device_id=device(px, py, z, k), device_id_type=MESH,
         )
 
-    def scatter(g, part, got, land):
-        copy = to_sibling(g, part, got)
-        copy.wait()
-        for row in range(NY):
-            got[row] = got[row] + part[k, row]
-
+    def scatter(g, got, land):
         def send(o, carry):
             scatter_copy(g, got, land, o).start()
             return carry
@@ -178,7 +205,7 @@
         )
 
     def own_along_y():
-        to_sibling(0, p_own, k_own).wait()
+        to_sibling().wait()
         for row in range(NY):
             k_own[row] = k_own[row] + p_own[k, row]
         for o in range(1, NY):
@@ -194,56 +221,92 @@
         r_own[x] = s_own[x]
 
     load.wait()
+    swap_own.start()
     put(p_own, 0, gram(own[:, :BS], own[:, :BS]))
     put(p_own, 1, gram(own[:, :BS], own[:, BS:]))
     put(p_own, 2, gram(own[:, BS:], own[:, BS:]))
-    to_sibling(0, p_own, k_own).start()
+    to_sibling().start()
 
     for j in range(CHUNKS):
         x_arrival(1, j).wait_recv()
         forward(j).start()
-        x_copy(0, j).wait_send()
-        x_copy(1, j).wait_send()
-        if j + WINDOW < CHUNKS:
-            x_copy(0, j + WINDOW).start()
-            x_copy(1, j + WINDOW).start()
+        x_arrival(0, j).wait_recv()
+        if (j + 1) % (CHUNKS // PARTS) == 0:
+            g = j // (CHUNKS // PARTS)
+            swap_rows(g, 0).start()
+            swap_rows(g, 1).start()
+            swap_cols(g).start()
         if j == 0:
             own_along_y()
         if j == CHUNKS - 3:
             own_along_x()
-    for j in range(CHUNKS):
-        x_arrival(0, j).wait_recv()
     share_pairs.wait_recv()
     load_pairs.wait()
     far = pltpu.make_async_copy(pairs_far, pairs_all.at[1 - c], local_sem.at[2])
     far.start()
 
-    for i in range(2):
+    for g in range(PARTS):
+        swap_rows(g, 0).wait_recv()
+        swap_rows(g, 1).wait_recv()
+        swap_cols(g).wait_recv()
+
+    near_rows = jnp.concatenate([strip(cross, 0, k, 0)[...], strip(cross, 1, k, 0)[...]], axis=1)
+
+    def put_pairs(ref, near, far):
         for j in range(2):
-            put(p_mid, 1 + 2 * i + j, gram(cross[0, :, i * BS : (i + 1) * BS], cross[1, :, j * BS : (j + 1) * BS]))
+            cols = slice(j * BS, (j + 1) * BS)
+            both = gram(near_rows, near[:, cols]) + gram(far_rows[...], far[:, cols])
+            put(ref, j, both[: BS // 2])
+            put(ref, 2 + j, both[BS // 2 :])
+
+    put_pairs(p_mid, cross.at[1], far_cols)
+    scatter(0, p_mid, r_mid)
+
     edge.wait_recv()
-    put(p_mid, 0, gram(own[:, BS:], ahead[...]))
-    to_sibling(1, p_mid, k_mid).start()
-    scatter(1, p_mid, k_mid, r_mid)
-
-    for j in range(CHUNKS):
-        forward(j).wait_recv()
-    for i in range(2):
-        for j in range(2):
-            put(p_low, 2 * i + j, gram(cross[0, :, i * BS : (i + 1) * BS], below[:, j * BS : (j + 1) * BS]))
-    to_sibling(2, p_low, k_low).start()
-    scatter(2, p_low, k_low, r_low)
+    swap_ahead.start()
+    for g in range(PARTS):
+        for j in range(g * CHUNKS // PARTS, (g + 1) * CHUNKS // PARTS):
+            forward(j).wait_recv()
+        swap_below(g).start()
+    swap_own.wait_recv()
+    swap_ahead.wait_recv()
+    put(p_low, 4, gram(strip(own, 1, k)[...], ahead[...]) + gram(far_own[...], far_ahead[...]))
+    for g in range(PARTS):
+        swap_below(g).wait_recv()
+    put_pairs(p_low, below, far_below)
+    scatter(1, p_low, r_low)
 
     for o in range(1, NX):
         row_copy(o, (x + o) % NX).wait_recv()
     for side in range(2):
         table[3 * side : 3 * side + 3] = (r_own[2 * side] + r_own[2 * side + 1]).reshape(3, 8, BS)
-    collect(1, k_mid, r_mid)
+    collect(0, p_mid, r_mid)
+
+    def add(land, at):
+        def one(q, carry):
+            rows = pl.ds(pl.multiple_of(q * 8, 8), 8)
+            terms = [land[source, rows, :] for source in range(CHIPS)]
+            while len(terms) > 1:
+                terms = [a + b for a, b in zip(terms[::2], terms[1::2])]
+            table[at + q] = terms[0]
+            return carry
+
+        lax.fori_loop(0, 4, one, 0)
+
+    add(r_mid, 8)
+    collect(1, p_low, r_low)
+    add(r_low, 12)
+    hop_down = pltpu.make_async_remote_copy(
+        src_ref=table.at[pl.ds(12, 4)], dst_ref=table.at[pl.ds(16, 4)],
+        send_sem=hop_send.at[1], recv_sem=hop_recv.at[1],
+        device_id=device(x, y, down, k), device_id_type=MESH,
+    )
+    hop_down.start()
     for side in range(2):
         total = None
         for row in range(NY):
             for col in range(2):
-                term = r_mid[row * NX + 2 * side + col, 0:8, :]
+                term = r_low[row * NX + 2 * side + col, 32:40, :]
                 total = term if total is None else total + term
         table[6 + side] = total
     hop_up = pltpu.make_async_remote_copy(
@@ -252,21 +315,6 @@
         device_id=device(x, y, up, k), device_id_type=MESH,
     )
     hop_up.start()
-    total = r_mid[0, 8:40, :]
-    for source in range(1, CHIPS):
-        total = total + r_mid[source, 8:40, :]
-    table[8:12] = total.reshape(4, 8, BS)
-    collect(2, k_low, r_low)
-    total = r_low[0]
-    for source in range(1, CHIPS):
-        total = total + r_low[source]
-    table[12:16] = total.reshape(4, 8, BS)
-    hop_down = pltpu.make_async_remote_copy(
-        src_ref=table.at[pl.ds(12, 4)], dst_ref=table.at[pl.ds(16, 4)],
-        send_sem=hop_send.at[1], recv_sem=hop_recv.at[1],
-        device_id=device(x, y, down, k), device_id_type=MESH,
-    )
-    hop_down.start()
     far.wait()
     hop_up.wait()
     hop_down.wait()
@@ -322,14 +370,23 @@
         out_ref[0, s] = jnp.where(slot < counts_ref[0], block * weight, 0.0)
 
     for j in range(CHUNKS):
+        x_copy(0, j).wait_send()
+        x_copy(1, j).wait_send()
         forward(j).wait_send()
+    for g in range(PARTS):
+        swap_rows(g, 0).wait_send()
+        swap_rows(g, 1).wait_send()
+        swap_cols(g).wait_send()
+        swap_below(g).wait_send()
+    swap_own.wait_send()
+    swap_ahead.wait_send()
     for o in range(1, NY):
         y_copy(o, y).wait_send()
     for o in range(1, NX):
         row_copy(o, x).wait_send()
     edge.wait_send()
     share_pairs.wait_send()
-    for g, got, land in ((1, k_mid, r_mid), (2, k_low, r_low)):
+    for g, got, land in ((0, p_mid, r_mid), (1, p_low, r_low)):
         def left(o, carry):
             scatter_copy(g, got, land, o).wait_send()
             return carry
@@ -355,10 +412,16 @@
         vmem((rows // 2, columns), bf16),
         vmem((rows, BS), bf16),
     ]
-    heights = (24, 40, 32)
-    scratch += [vmem((2, NY, NX, h, BS), f32) for h in heights]
-    scratch += [vmem((NY, NX, h, BS), f32) for h in heights]
-    scratch += [vmem((n, h, BS), f32) for n, h in zip((NX, CHIPS, CHIPS), heights)]
+    scratch += [
+        vmem((rows // 2, BS), bf16),
+        vmem((rows // 2, columns), bf16),
+        vmem((rows // 2, columns), bf16),
+        vmem((rows, BS // 2), bf16),
+        vmem((rows, BS), bf16),
+        vmem((2, NY, NX, 24, BS), f32), vmem((NY, NX, 24, BS), f32),
+        vmem((NY, NX, 32, BS), f32), vmem((NY, NX, 40, BS), f32),
+        vmem((NX, 24, BS), f32), vmem((CHIPS, 32, BS), f32), vmem((CHIPS, 40, BS), f32),
+    ]
     scratch += [
         vmem((22, 8, BS), f32),
         vmem((2 * CHIPS, slots, 8, BS), f32),
@@ -370,10 +433,10 @@
         dma((2, CHUNKS)), dma((2, CHUNKS)),
         dma((CHUNKS,)), dma((CHUNKS,)),
         dma, dma, dma, dma,
-        dma((3,)), dma((3,)),
-        vmem((NY, NX, heights[0], BS), f32), vmem((NX, heights[0], BS), f32),
+        dma, dma, dma((4 * PARTS + 2,)), dma((4 * PARTS + 2,)),
+        vmem((NY, NX, 24, BS), f32), vmem((NX, 24, BS), f32),
         dma((NY,)), dma((NY,)), dma((NX,)), dma((NX,)),
-        dma((3, CHIPS)), dma((3, CHIPS)),
+        dma((2, CHIPS)), dma((2, CHIPS)),
         dma((2,)), dma((2,)),
         dma((2 * CHIPS,)), dma((2 * CHIPS,)),
     ]
@@ -388,7 +451,7 @@
         out_specs=pl.BlockSpec(memory_space=pltpu.VMEM),
         scratch_shapes=scratch,
         compiler_params=pltpu.CompilerParams(
-            collective_id=0, has_side_effects=True, vmem_limit_bytes=62 * 2**20
+            collective_id=0, has_side_effects=True, vmem_limit_bytes=252 * 2**18
         ),
     )(layer_input, pairs, counts)
 

time: 59.2 us -> 59.7 us (level)
  no operation moved by 1% of the time
where the time goes in v3:
time: 59.7 us; the launch traced here: 59.5 us
  Pallas kernels  57 us (95%)
  local copies, waits for them, and re-layouts  1.87 us (3%)
  between operations  0.66 us (1%)
    pallas_call x1, Pallas kernels, shards(): pl.pallas_call(functools.partial(kernel, weight), out_shape=jax.ShapeDtyp...  57 us
    unnamed x1, local copies, waits for them, and re-layouts  1.87 us

profile of v3, /device:TPU:1, one launch (start us, length us, event | category | flops | bytes accessed | tf_op | source)
XLA Modules:
  0.0 59.5 jit_solution(6228100201565407940)
XLA Ops:
  0.7 57.0 %shard_map.37 = f32[1,2,256,256]{3,2,1,0:T(8,128)} custom-call(bf16[1024,512]{1,0:T(8,128)(2,1)} %x_ref.1, s32[2,1,32]{2,1,0:T(1,128)} %pairs_ref.1, s32[1]{0:T(128)S(6)} %copy.5.counts_ref), custom_call_target="tpu_custom_call" | custom-call | tf_op jit(solution)/shard_map/pallas_call | solution.py:443
  57.7 1.9 %copy.6 = f32[1,2,256,256]{3,2,1,0:T(8,128)} copy(f32[1,2,256,256]{3,2,1,0:T(8,128)} %shard_map.37) | data formatting | bytes 1048576

commit v4 on v3

--- a/solution.py
+++ b/solution.py
@@ -36,10 +36,26 @@
     return lax.dot_general(a, b, (((0,), (0,)), ((), ())), preferred_element_type=jnp.float32)
 
 
+def exponents(peak):
+    return jnp.ceil(8.0 * jnp.log2(jnp.maximum(peak, 1e-30) * (1.0 / 32000.0)))
+
+
+def spread(rows):
+    return jnp.concatenate([jnp.broadcast_to(row, (8, BS)) for row in rows], axis=0)
+
+
+def to_i16(value):
+    return jnp.floor(value + 0.5).astype(jnp.int32).astype(jnp.int16)
+
+
+def to_f32(value):
+    return value.astype(jnp.int32).astype(jnp.float32)
+
+
 def kernel(
     weight, x_ref, pairs_ref, counts_ref, out_ref,
     own, cross, below, ahead, far_rows, far_cols, far_below, far_own, far_ahead,
-    p_own, k_own, p_mid, p_low, r_own, r_mid, r_low, table, stage, arrived, pairs_far, pairs_all, lookup,
+    p_own, k_own, p_mid, p_low, q_mid, q_low, scales, r_own, r_mid, r_low, grow, table, stage, arrived, pairs_far, pairs_all, lookup,
     local_sem, x_send, x_recv, zf_send, zf_recv, ze_send, ze_recv, pr_send, pr_recv,
     core_send, core_recv, swap_send, swap_recv, y_own, s_own, y_send, y_recv, row_send, row_recv, rs_send, rs_recv, hop_send, hop_recv, out_send, out_recv,
 ):
@@ -260,7 +276,23 @@
             put(ref, 2 + j, both[BS // 2 :])
 
     put_pairs(p_mid, cross.at[1], far_cols)
-    scatter(0, p_mid, r_mid)
+
+    def peak(ref, q):
+        top = None
+        for row in range(NY):
+            for col in range(NX):
+                size = jnp.abs(ref[row, col, q * 8 : q * 8 + 8, :])
+                top = size if top is None else jnp.maximum(top, size)
+        return jnp.max(top, axis=0, keepdims=True)
+
+    rows = [exponents(peak(p_mid, q)) for q in range(4)]
+    for q in range(4):
+        scales[q : q + 1, :] = rows[q]
+    shrink = spread([jnp.exp2(row * -0.125) for row in rows])
+    for row in range(NY):
+        for col in range(NX):
+            q_mid[row, col] = to_i16(p_mid[row, col] * shrink)
+    scatter(0, q_mid, r_mid)
 
     edge.wait_recv()
     swap_ahead.start()
@@ -274,47 +306,52 @@
     for g in range(PARTS):
         swap_below(g).wait_recv()
     put_pairs(p_low, below, far_below)
-    scatter(1, p_low, r_low)
+    rows = [exponents(jnp.maximum(peak(p_low, q), peak(p_low, 2 + q))) for q in range(2)]
+    rows.append(exponents(peak(p_low, 4)))
+    for q in range(3):
+        scales[4 + q : 5 + q, :] = rows[q]
+    scales[7:8, :] = jnp.zeros((1, BS), jnp.float32)
+    shrink = spread([jnp.exp2(rows[q] * -0.125) for q in (0, 1, 0, 1, 2)])
+    for row in range(NY):
+        for col in range(NX):
+            q_low[row, col] = to_i16(jnp.concatenate([p_low[row, col] * shrink, scales[...]], axis=0))
+    scatter(1, q_low, r_low)
 
     for o in range(1, NX):
         row_copy(o, (x + o) % NX).wait_recv()
     for side in range(2):
         table[3 * side : 3 * side + 3] = (r_own[2 * side] + r_own[2 * side + 1]).reshape(3, 8, BS)
-    collect(0, p_mid, r_mid)
-
-    def add(land, at):
-        def one(q, carry):
-            rows = pl.ds(pl.multiple_of(q * 8, 8), 8)
-            terms = [land[source, rows, :] for source in range(CHIPS)]
-            while len(terms) > 1:
-                terms = [a + b for a, b in zip(terms[::2], terms[1::2])]
-            table[at + q] = terms[0]
-            return carry
-
-        lax.fori_loop(0, 4, one, 0)
-
-    add(r_mid, 8)
-    collect(1, p_low, r_low)
-    add(r_low, 12)
+    collect(1, q_low, r_low)
+    edges, sums = [None, None], None
+    for source in range(CHIPS):
+        tail = to_f32(r_low[source, 32:48, :])
+        grow[source] = jnp.exp2(tail[8:16, :] * 0.125)
+        term = to_f32(r_low[source, 0:32, :]) * spread([grow[source, q : q + 1, :] for q in (4, 5, 4, 5)])
+        sums = term if sums is None else sums + term
+        edge_term = tail[0:8, :] * grow[source, 6:7, :]
+        side = source % NX // 2
+        edges[side] = edge_term if edges[side] is None else edges[side] + edge_term
+    table[12:16] = sums.reshape(4, 8, BS)
     hop_down = pltpu.make_async_remote_copy(
         src_ref=table.at[pl.ds(12, 4)], dst_ref=table.at[pl.ds(16, 4)],
         send_sem=hop_send.at[1], recv_sem=hop_recv.at[1],
         device_id=device(x, y, down, k), device_id_type=MESH,
     )
     hop_down.start()
-    for side in range(2):
-        total = None
-        for row in range(NY):
-            for col in range(2):
-                term = r_low[row * NX + 2 * side + col, 32:40, :]
-                total = term if total is None else total + term
-        table[6 + side] = total
+    table[6] = edges[0]
+    table[7] = edges[1]
     hop_up = pltpu.make_async_remote_copy(
         src_ref=table.at[pl.ds(6, 2)], dst_ref=table.at[pl.ds(20, 2)],
         send_sem=hop_send.at[0], recv_sem=hop_recv.at[0],
         device_id=device(x, y, up, k), device_id_type=MESH,
     )
     hop_up.start()
+    collect(0, q_mid, r_mid)
+    sums = None
+    for source in range(CHIPS):
+        term = to_f32(r_mid[source]) * spread([grow[source, q : q + 1, :] for q in range(4)])
+        sums = term if sums is None else sums + term
+    table[8:12] = sums.reshape(4, 8, BS)
     far.wait()
     hop_up.wait()
     hop_down.wait()
@@ -386,7 +423,7 @@
         row_copy(o, x).wait_send()
     edge.wait_send()
     share_pairs.wait_send()
-    for g, got, land in ((0, p_mid, r_mid), (1, p_low, r_low)):
+    for g, got, land in ((0, q_mid, r_mid), (1, q_low, r_low)):
         def left(o, carry):
             scatter_copy(g, got, land, o).wait_send()
             return carry
@@ -404,7 +441,7 @@
     rows, columns = layer_input.shape
     weight = 2.0 / (rows * lax.axis_size("token"))
     dma, vmem = pltpu.SemaphoreType.DMA, pltpu.VMEM
-    f32, bf16 = jnp.float32, jnp.bfloat16
+    f32, bf16, i16 = jnp.float32, jnp.bfloat16, jnp.int16
     slots = pairs.shape[2] // lax.axis_size("token")
     scratch = [
         vmem((rows, columns), bf16),
@@ -420,7 +457,9 @@
         vmem((rows, BS), bf16),
         vmem((2, NY, NX, 24, BS), f32), vmem((NY, NX, 24, BS), f32),
         vmem((NY, NX, 32, BS), f32), vmem((NY, NX, 40, BS), f32),
-        vmem((NX, 24, BS), f32), vmem((CHIPS, 32, BS), f32), vmem((CHIPS, 40, BS), f32),
+        vmem((NY, NX, 32, BS), i16), vmem((NY, NX, 48, BS), i16), vmem((8, BS), f32),
+        vmem((NX, 24, BS), f32), vmem((CHIPS, 32, BS), i16), vmem((CHIPS, 48, BS), i16),
+        vmem((CHIPS, 8, BS), f32),
     ]
     scratch += [
         vmem((22, 8, BS), f32),

time: 59.7 us -> 53.8 us (0.901)
  Pallas kernels: 57 us -> 51.1 us
    pallas_call x1, Pallas kernels: 57 us -> 51.1 us  [shards(): pl.pallas_call(functools.partial(kernel, weight), out_shape=jax.ShapeDtyp...]
where the time goes in v4:
time: 53.8 us; the launch traced here: 53.6 us
  Pallas kernels  51.1 us (95%)
  local copies, waits for them, and re-layouts  1.87 us (3%)
  between operations  0.66 us (1%)
    pallas_call x1, Pallas kernels, shards(): pl.pallas_call(functools.partial(kernel, weight), out_shape=jax.ShapeDtyp...  51.1 us
    unnamed x1, local copies, waits for them, and re-layouts  1.87 us

profile of v4, /device:TPU:1, one launch (start us, length us, event | category | flops | bytes accessed | tf_op | source)
XLA Modules:
  0.0 53.6 jit_solution(4149022317465749489)
XLA Ops:
  0.7 51.1 %shard_map.37 = f32[1,2,256,256]{3,2,1,0:T(8,128)} custom-call(bf16[1024,512]{1,0:T(8,128)(2,1)} %x_ref.1, s32[2,1,32]{2,1,0:T(1,128)} %pairs_ref.1, s32[1]{0:T(128)S(6)} %copy.5.counts_ref), custom_call_target="tpu_custom_call" | custom-call | tf_op jit(solution)/shard_map/pallas_call | solution.py:482
  51.8 1.9 %copy.6 = f32[1,2,256,256]{3,2,1,0:T(8,128)} copy(f32[1,2,256,256]{3,2,1,0:T(8,128)} %shard_map.37) | data formatting | bytes 1048576

commit v5 on v4

--- a/solution.py
+++ b/solution.py
@@ -36,6 +36,10 @@
     return lax.dot_general(a, b, (((0,), (0,)), ((), ())), preferred_element_type=jnp.float32)
 
 
+def far_first(n):
+    return (2 + 3 * n + 3 * (n * (n - 1) // 2)) % 4
+
+
 def exponents(peak):
     return jnp.ceil(8.0 * jnp.log2(jnp.maximum(peak, 1e-30) * (1.0 / 32000.0)))
 
@@ -55,7 +59,7 @@
 def kernel(
     weight, x_ref, pairs_ref, counts_ref, out_ref,
     own, cross, below, ahead, far_rows, far_cols, far_below, far_own, far_ahead,
-    p_own, k_own, p_mid, p_low, q_mid, q_low, scales, r_own, r_mid, r_low, grow, table, stage, arrived, pairs_far, pairs_all, lookup,
+    p_own, k_own, p_mid, p_low, q_mid, q_low, scales, r_own, r_mid, r_low, grow, table, packed, blocks, stage, arrived, pairs_far, pairs_all, lookup,
     local_sem, x_send, x_recv, zf_send, zf_recv, ze_send, ze_recv, pr_send, pr_recv,
     core_send, core_recv, swap_send, swap_recv, y_own, s_own, y_send, y_recv, row_send, row_recv, rs_send, rs_recv, hop_send, hop_recv, out_send, out_recv,
 ):
@@ -77,8 +81,11 @@
 
     barrier = pltpu.get_barrier_semaphore()
 
+    def chip_peer(o):
+        return (x + far_first(o % NX)) % NX, (y + far_first(o // NX)) % NY
+
     def plane_peer(o):
-        return (x + o % NX) % NX, (y + (o // NX) % NY) % NY, (k + o // CHIPS) % 2
+        return chip_peer(o // 2) + ((k + 1 - o % 2) % 2,)
 
     near = [device((x + o) % NX, y, z, k) for o in (2, 1, 3)]
     near += [device(x, (y + o) % NY, z, k) for o in (2, 1, 3)]
@@ -175,7 +182,7 @@
         )
 
     def scatter_copy(g, got, land, o):
-        px, py = (x + o % NX) % NX, (y + o // NX) % NY
+        px, py = chip_peer(o)
         return pltpu.make_async_remote_copy(
             src_ref=got.at[py, px], dst_ref=land.at[me],
             send_sem=rs_send.at[g, o], recv_sem=rs_recv.at[g, me],
@@ -183,7 +190,7 @@
         )
 
     def scatter_arrival(g, got, land, o):
-        px, py = (x + o % NX) % NX, (y + o // NX) % NY
+        px, py = chip_peer(o)
         source = py * NX + px
         return pltpu.make_async_remote_copy(
             src_ref=got.at[py, px], dst_ref=land.at[source],
@@ -196,7 +203,7 @@
             scatter_copy(g, got, land, o).start()
             return carry
 
-        lax.fori_loop(1, CHIPS, send, 0)
+        lax.fori_loop(0, CHIPS - 1, send, 0)
         land[me] = got[y, x]
 
     def collect(g, got, land):
@@ -204,7 +211,7 @@
             scatter_arrival(g, got, land, o).wait_recv()
             return carry
 
-        lax.fori_loop(1, CHIPS, take, 0)
+        lax.fori_loop(0, CHIPS - 1, take, 0)
 
     def y_copy(o, source):
         return pltpu.make_async_remote_copy(
@@ -352,9 +359,17 @@
         term = to_f32(r_mid[source]) * spread([grow[source, q : q + 1, :] for q in range(4)])
         sums = term if sums is None else sums + term
     table[8:12] = sums.reshape(4, 8, BS)
+    def pack(first, count):
+        value = table[first : first + count]
+        scale = exponents(jnp.max(jnp.abs(value), axis=2, keepdims=True))
+        packed[first : first + count, :, :BS] = value * jnp.exp2(scale * -0.125)
+        packed[first : first + count, :, BS:] = jnp.broadcast_to(scale, (count, 8, 128))
+
+    pack(0, 16)
     far.wait()
     hop_up.wait()
     hop_down.wait()
+    pack(16, 6)
 
     def code(reader, slot):
         row = pairs_all[reader, 0, 0, slot]
@@ -365,8 +380,8 @@
     def fill(o, px, py, pk):
         slot = 2 * (((px % 2) * NY + py) * 2 + pk)
         reader = px // 2
-        stage[o, 0] = table[code(reader, slot) // 2]
-        stage[o, 1] = table[code(reader, slot + 1) // 2]
+        both = [packed[code(reader, slot + s) // 2] for s in range(2)]
+        stage[o] = to_i16(jnp.concatenate(both, axis=0))
 
     rank = k * CHIPS + me
 
@@ -384,9 +399,9 @@
         deliver(o).start()
         return carry
 
-    lax.fori_loop(1, 2 * CHIPS, send_out, 0)
-    fill(0, x, y, k)
-    arrived[rank] = stage[0]
+    lax.fori_loop(0, 2 * CHIPS - 1, send_out, 0)
+    fill(2 * CHIPS - 1, x, y, k)
+    arrived[rank] = stage[2 * CHIPS - 1]
 
     def take_out(o, carry):
         px, py, pk = plane_peer(o)
@@ -398,10 +413,19 @@
         ).wait_recv()
         return carry
 
-    lax.fori_loop(1, 2 * CHIPS, take_out, 0)
+    lax.fori_loop(0, 2 * CHIPS - 1, take_out, 0)
+    def unpack(source, carry):
+        value = to_f32(arrived[source])
+        scale = jnp.exp2(value[:, BS:] * 0.125)
+        value = value[:, :BS] * jnp.concatenate([scale, scale], axis=1)
+        blocks[0, source] = value[:8]
+        blocks[1, source] = value[8:]
+        return carry
+
+    lax.fori_loop(0, 2 * CHIPS, unpack, 0)
     for s in range(2):
         slot = 2 * token + s
-        block = arrived[:, s].reshape(BS, BS)
+        block = blocks[s].reshape(BS, BS)
         flip = code(c, slot) % 2 == 1
         block = jnp.where(flip, block.T, block)
         out_ref[0, s] = jnp.where(slot < counts_ref[0], block * weight, 0.0)
@@ -428,13 +452,13 @@
             scatter_copy(g, got, land, o).wait_send()
             return carry
 
-        lax.fori_loop(1, CHIPS, left, 0)
+        lax.fori_loop(0, CHIPS - 1, left, 0)
 
     def left_out(o, carry):
         deliver(o).wait_send()
         return carry
 
-    lax.fori_loop(1, 2 * CHIPS, left_out, 0)
+    lax.fori_loop(0, 2 * CHIPS - 1, left_out, 0)
 
 
 def shards(layer_input, pairs, counts):
@@ -463,8 +487,10 @@
     ]
     scratch += [
         vmem((22, 8, BS), f32),
-        vmem((2 * CHIPS, slots, 8, BS), f32),
-        vmem((2 * CHIPS, slots, 8, BS), f32),
+        vmem((22, 8, BS + 128), f32),
+        vmem((slots, 2 * CHIPS, 8, BS), f32),
+        vmem((2 * CHIPS, 8 * slots, BS + 128), i16),
+        vmem((2 * CHIPS, 8 * slots, BS + 128), i16),
         vmem(pairs.shape, jnp.int32),
         pltpu.SMEM((2,) + pairs.shape, jnp.int32),
         pltpu.SMEM((BAND * WIDTH,), jnp.int32),
@@ -490,7 +516,7 @@
         out_specs=pl.BlockSpec(memory_space=pltpu.VMEM),
         scratch_shapes=scratch,
         compiler_params=pltpu.CompilerParams(
-            collective_id=0, has_side_effects=True, vmem_limit_bytes=252 * 2**18
+            collective_id=0, has_side_effects=True, vmem_limit_bytes=211 * 2**18
         ),
     )(layer_input, pairs, counts)
 

time: 53.8 us -> 50.1 us (0.931)
  Pallas kernels: 51.1 us -> 48.5 us
  local copies, waits for them, and re-layouts: 1.87 us -> 0.81 us
    pallas_call x1, Pallas kernels: 51.1 us -> 48.5 us  [shards(): pl.pallas_call(functools.partial(kernel, weight), out_shape=jax.ShapeDtyp...]
    unnamed x1 -> x3, local copies, waits for them, and re-layouts: 1.87 us -> 0.81 us
where the time goes in v5:
time: 50.1 us; the launch traced here: 50 us
  Pallas kernels  48.5 us (97%)
  local copies, waits for them, and re-layouts  0.81 us (2%)
  between operations  0.68 us (1%)
    pallas_call x1, Pallas kernels, shards(): pl.pallas_call(functools.partial(kernel, weight), out_shape=jax.ShapeDtyp...  48.5 us

profile of v5, /device:TPU:1, one launch (start us, length us, event | category | flops | bytes accessed | tf_op | source)
XLA Modules:
  0.0 50.0 jit_solution(13033046585496791881)
XLA Ops:
  0.0 0.0 copy-start
  0.7 0.0 copy-done
  0.7 48.5 %shard_map.37 = f32[1,2,256,256]{3,2,1,0:T(8,128)S(1)} custom-call(bf16[1024,512]{1,0:T(8,128)(2,1)} %x_ref.1, s32[2,1,32]{2,1,0:T(1,128)S(1)} %copy-done, s32[1]{0:T(128)S(6)} %copy.5.counts_ref), custom_call_target="tpu_custom_call" | custom-call | tf_op jit(solution)/shard_map/pallas_call | solution.py:508
  49.2 0.8 %copy.6 = f32[1,2,256,256]{3,2,1,0:T(8,128)} copy(f32[1,2,256,256]{3,2,1,0:T(8,128)S(1)} %shard_map.37) | data formatting | bytes 1048576
Async XLA Ops:
  0.0 0.7 %copy-start = (s32[2,1,32]{2,1,0:T(1,128)S(1)}, s32[2,1,32]{2,1,0:T(1,128)}, u32[]{:S(2)}) copy-start(s32[2,1,32]{2,1,0:T(1,128)} %pairs_ref.1) | copy-start | bytes 772

commit v6 on v5

--- a/solution.py
+++ b/solution.py
@@ -12,6 +12,7 @@
 CHIPS = NX * NY
 CHUNKS = 8
 PARTS = 4
+FULL = 32000.0
 MESH = pl.DeviceIdType.MESH
 
 TABLE = {
@@ -41,11 +42,20 @@
 
 
 def exponents(peak):
-    return jnp.ceil(8.0 * jnp.log2(jnp.maximum(peak, 1e-30) * (1.0 / 32000.0)))
+    return jnp.ceil(8.0 * jnp.log2(jnp.maximum(peak, 1e-30)))
 
 
 def spread(rows):
-    return jnp.concatenate([jnp.broadcast_to(row, (8, BS)) for row in rows], axis=0)
+    return jnp.concatenate([jnp.broadcast_to(row, (8, row.shape[1])) for row in rows], axis=0)
+
+
+def compress(value):
+    root = FULL * jnp.sqrt(jnp.abs(value))
+    return jnp.where(value < 0.0, -root, root)
+
+
+def expand(coded):
+    return coded * jnp.abs(coded) * (1.0 / (FULL * FULL))
 
 
 def to_i16(value):
@@ -58,8 +68,8 @@
 
 def kernel(
     weight, x_ref, pairs_ref, counts_ref, out_ref,
-    own, cross, below, ahead, far_rows, far_cols, far_below, far_own, far_ahead,
-    p_own, k_own, p_mid, p_low, q_mid, q_low, scales, r_own, r_mid, r_low, grow, table, packed, blocks, stage, arrived, pairs_far, pairs_all, lookup,
+    own, cross, below, ahead, far_rows, far_cols, far_below,
+    p_own, k_own, rows_t, sums_low, p_mid, p_low, p_edge, k_edge, q_mid, q_low, q_edge, scales, scales_low, r_own, r_mid, r_low, r_edge, grow, factor, table, packed, blocks, stage, arrived, pairs_far, pairs_all, lookup, codes,
     local_sem, x_send, x_recv, zf_send, zf_recv, ze_send, ze_recv, pr_send, pr_recv,
     core_send, core_recv, swap_send, swap_recv, y_own, s_own, y_send, y_recv, row_send, row_recv, rs_send, rs_recv, hop_send, hop_recv, out_send, out_recv,
 ):
@@ -146,10 +156,6 @@
             device_id=device(x, y, z, 1 - k), device_id_type=MESH,
         )
 
-    def strip(ref, block, core, *lead):
-        first = pl.multiple_of(block * BS + core * (BS // 2), BS // 2)
-        return ref.at[lead + (slice(None), pl.ds(first, BS // 2))]
-
     part = half // PARTS
 
     def swap_rows(g, i):
@@ -168,16 +174,13 @@
         rows = pl.ds(g * part, part)
         return swap(3 * PARTS + g, below.at[rows, :], far_below.at[rows, :])
 
-    swap_own = swap(4 * PARTS, strip(own, 1, 1 - k), far_own)
-    swap_ahead = swap(4 * PARTS + 1, ahead, far_ahead)
-
     def put(ref, q, value):
         ref[..., q * 8 : q * 8 + 8, :] = value.reshape(ref.shape[:-2] + (8, BS))
 
-    def to_sibling():
-        return pltpu.make_async_remote_copy(
-            src_ref=p_own.at[1 - k], dst_ref=k_own,
-            send_sem=core_send, recv_sem=core_recv,
+    def to_sibling(n, ref, got):
+        return pltpu.make_async_remote_copy(
+            src_ref=ref.at[1 - k], dst_ref=got,
+            send_sem=core_send.at[n], recv_sem=core_recv.at[n],
             device_id=device(x, y, z, 1 - k), device_id_type=MESH,
         )
 
@@ -198,13 +201,15 @@
             device_id=device(px, py, z, k), device_id_type=MESH,
         )
 
-    def scatter(g, got, land):
+    def scatter(g, encode, got, land):
         def send(o, carry):
+            px, py = chip_peer(o)
+            got[py, px] = encode(py, px)
             scatter_copy(g, got, land, o).start()
             return carry
 
         lax.fori_loop(0, CHIPS - 1, send, 0)
-        land[me] = got[y, x]
+        land[me] = encode(y, x)
 
     def collect(g, got, land):
         def take(o, carry):
@@ -228,7 +233,7 @@
         )
 
     def own_along_y():
-        to_sibling().wait()
+        to_sibling(0, p_own, k_own).wait()
         for row in range(NY):
             k_own[row] = k_own[row] + p_own[k, row]
         for o in range(1, NY):
@@ -244,25 +249,34 @@
         r_own[x] = s_own[x]
 
     load.wait()
-    swap_own.start()
     put(p_own, 0, gram(own[:, :BS], own[:, :BS]))
     put(p_own, 1, gram(own[:, :BS], own[:, BS:]))
     put(p_own, 2, gram(own[:, BS:], own[:, BS:]))
-    to_sibling().start()
+    to_sibling(0, p_own, k_own).start()
+
+    per_part = CHUNKS // PARTS
+
+    def pass_below(g):
+        for j in range(g * per_part, (g + 1) * per_part):
+            forward(j).wait_recv()
+        swap_below(g).start()
 
     for j in range(CHUNKS):
         x_arrival(1, j).wait_recv()
         forward(j).start()
         x_arrival(0, j).wait_recv()
-        if (j + 1) % (CHUNKS // PARTS) == 0:
-            g = j // (CHUNKS // PARTS)
+        if j == 0:
+            own_along_y()
+        if (j + 1) % per_part == 0:
+            g = j // per_part
             swap_rows(g, 0).start()
             swap_rows(g, 1).start()
             swap_cols(g).start()
-        if j == 0:
-            own_along_y()
-        if j == CHUNKS - 3:
-            own_along_x()
+            tokens = slice(g * part, (g + 1) * part)
+            near = [cross[0, tokens, pl.ds(pl.multiple_of(i * BS + k * (BS // 2), BS // 2), BS // 2)] for i in range(2)]
+            rows_t[:, tokens] = jnp.concatenate(near, axis=1).T
+            if g >= 2:
+                pass_below(g - 2)
     share_pairs.wait_recv()
     load_pairs.wait()
     far = pltpu.make_async_copy(pairs_far, pairs_all.at[1 - c], local_sem.at[2])
@@ -271,18 +285,19 @@
     for g in range(PARTS):
         swap_rows(g, 0).wait_recv()
         swap_rows(g, 1).wait_recv()
+        rows_t[:, half + g * part : half + (g + 1) * part] = far_rows[g * part : (g + 1) * part, :].T
         swap_cols(g).wait_recv()
 
-    near_rows = jnp.concatenate([strip(cross, 0, k, 0)[...], strip(cross, 1, k, 0)[...]], axis=1)
-
-    def put_pairs(ref, near, far):
-        for j in range(2):
-            cols = slice(j * BS, (j + 1) * BS)
-            both = gram(near_rows, near[:, cols]) + gram(far_rows[...], far[:, cols])
-            put(ref, j, both[: BS // 2])
-            put(ref, 2 + j, both[BS // 2 :])
-
-    put_pairs(p_mid, cross.at[1], far_cols)
+    def product(near, far_part, first, last, cols):
+        return jnp.dot(
+            rows_t[:, first:last], near[first:last, cols], preferred_element_type=jnp.float32
+        ) + jnp.dot(
+            rows_t[:, half + first : half + last], far_part[first:last, cols], preferred_element_type=jnp.float32
+        )
+
+    def put_pairs(ref, j, both):
+        put(ref, j, both[: BS // 2])
+        put(ref, 2 + j, both[BS // 2 :])
 
     def peak(ref, q):
         top = None
@@ -292,59 +307,90 @@
                 top = size if top is None else jnp.maximum(top, size)
         return jnp.max(top, axis=0, keepdims=True)
 
+    for j in range(2):
+        put_pairs(p_mid, j, product(cross.at[1], far_cols, 0, half, slice(j * BS, (j + 1) * BS)))
     rows = [exponents(peak(p_mid, q)) for q in range(4)]
+    scales[...] = jnp.zeros_like(scales)
     for q in range(4):
         scales[q : q + 1, :] = rows[q]
-    shrink = spread([jnp.exp2(row * -0.125) for row in rows])
-    for row in range(NY):
-        for col in range(NX):
-            q_mid[row, col] = to_i16(p_mid[row, col] * shrink)
-    scatter(0, q_mid, r_mid)
-
+    grow[0:32, :] = spread([jnp.exp2(row * -0.125) for row in rows])
+    scatter(0, lambda row, col: to_i16(compress(p_mid[row, col] * grow[0:32, :])), q_mid, r_mid)
+
+    pass_below(PARTS - 2)
     edge.wait_recv()
-    swap_ahead.start()
-    for g in range(PARTS):
-        for j in range(g * CHUNKS // PARTS, (g + 1) * CHUNKS // PARTS):
-            forward(j).wait_recv()
-        swap_below(g).start()
-    swap_own.wait_recv()
-    swap_ahead.wait_recv()
-    put(p_low, 4, gram(strip(own, 1, k)[...], ahead[...]) + gram(far_own[...], far_ahead[...]))
-    for g in range(PARTS):
+    put(p_edge, 0, gram(own[:, BS:], ahead[...]))
+    to_sibling(1, p_edge, k_edge).start()
+    own_along_x()
+    early = half - part
+    for g in range(PARTS - 1):
         swap_below(g).wait_recv()
-    put_pairs(p_low, below, far_below)
+    for j in range(2):
+        cols = slice(j * BS, (j + 1) * BS)
+        sums_low[:, cols] = product(below, far_below, 0, early, cols)
+    to_sibling(1, p_edge, k_edge).wait()
+    k_edge[...] = k_edge[...] + p_edge[k]
+    row = exponents(peak(k_edge, 0))
+    scales[4:5, :] = row
+    grow[32:40, :] = spread([jnp.exp2(row * -0.125)])
+
+    def encode_edge(row, col):
+        coded = compress(k_edge[row, col] * grow[32:40, :])
+        return to_i16(jnp.concatenate([coded, scales[...]], axis=0))
+
+    scatter(2, encode_edge, q_edge, r_edge)
+    pass_below(PARTS - 1)
+    swap_below(PARTS - 1).wait_recv()
+    for j in range(2):
+        cols = slice(j * BS, (j + 1) * BS)
+        put_pairs(p_low, j, sums_low[:, cols] + product(below, far_below, early, half, cols))
     rows = [exponents(jnp.maximum(peak(p_low, q), peak(p_low, 2 + q))) for q in range(2)]
-    rows.append(exponents(peak(p_low, 4)))
-    for q in range(3):
-        scales[4 + q : 5 + q, :] = rows[q]
-    scales[7:8, :] = jnp.zeros((1, BS), jnp.float32)
-    shrink = spread([jnp.exp2(rows[q] * -0.125) for q in (0, 1, 0, 1, 2)])
-    for row in range(NY):
-        for col in range(NX):
-            q_low[row, col] = to_i16(jnp.concatenate([p_low[row, col] * shrink, scales[...]], axis=0))
-    scatter(1, q_low, r_low)
+    scales_low[...] = jnp.zeros_like(scales_low)
+    for q in range(2):
+        for h in range(2):
+            scales_low[2 * q + h : 2 * q + h + 1, :] = rows[q][:, h * 128 : h * 128 + 128]
+    grow[40:72, :] = spread([jnp.exp2(rows[q] * -0.125) for q in (0, 1, 0, 1)])
+
+    def encode_low(row, col):
+        coded = compress(p_low[row, col] * grow[40:72, :])
+        return to_i16(jnp.concatenate([coded[:, :128], coded[:, 128:], scales_low[...]], axis=0))
+
+    scatter(1, encode_low, q_low, r_low)
+
+    far.wait()
+
+    def code(reader, slot):
+        row = pairs_all[reader, 0, 0, slot]
+        col = pairs_all[reader, 1, 0, slot]
+        at = (row - z * BAND) * WIDTH + col - row + BAND - 1
+        return lookup[jnp.clip(at, 0, BAND * WIDTH - 1)]
+
+    def note(o, carry):
+        px, py, pk = plane_peer(o)
+        slot = 2 * (((px % 2) * NY + py) * 2 + pk)
+        for s in range(2):
+            codes[2 * o + s] = code(px // 2, slot + s)
+        return carry
+
+    lax.fori_loop(0, 2 * CHIPS, note, 0)
 
     for o in range(1, NX):
         row_copy(o, (x + o) % NX).wait_recv()
     for side in range(2):
         table[3 * side : 3 * side + 3] = (r_own[2 * side] + r_own[2 * side + 1]).reshape(3, 8, BS)
-    collect(1, q_low, r_low)
-    edges, sums = [None, None], None
+    def pack(first, count):
+        value = table[first : first + count]
+        scale = exponents(jnp.max(jnp.abs(value), axis=2, keepdims=True))
+        packed[first : first + count, :, :BS] = compress(value * jnp.exp2(scale * -0.125))
+        packed[first : first + count, :, BS:] = jnp.broadcast_to(scale, (count, 8, 128))
+
+    collect(2, q_edge, r_edge)
+    edges = [None, None]
     for source in range(CHIPS):
-        tail = to_f32(r_low[source, 32:48, :])
-        grow[source] = jnp.exp2(tail[8:16, :] * 0.125)
-        term = to_f32(r_low[source, 0:32, :]) * spread([grow[source, q : q + 1, :] for q in (4, 5, 4, 5)])
-        sums = term if sums is None else sums + term
-        edge_term = tail[0:8, :] * grow[source, 6:7, :]
+        tail = to_f32(r_edge[source])
+        factor[source] = jnp.exp2(tail[8:16, :] * 0.125)
+        term = expand(tail[0:8, :]) * factor[source, 4:5, :]
         side = source % NX // 2
-        edges[side] = edge_term if edges[side] is None else edges[side] + edge_term
-    table[12:16] = sums.reshape(4, 8, BS)
-    hop_down = pltpu.make_async_remote_copy(
-        src_ref=table.at[pl.ds(12, 4)], dst_ref=table.at[pl.ds(16, 4)],
-        send_sem=hop_send.at[1], recv_sem=hop_recv.at[1],
-        device_id=device(x, y, down, k), device_id_type=MESH,
-    )
-    hop_down.start()
+        edges[side] = term if edges[side] is None else edges[side] + term
     table[6] = edges[0]
     table[7] = edges[1]
     hop_up = pltpu.make_async_remote_copy(
@@ -356,31 +402,36 @@
     collect(0, q_mid, r_mid)
     sums = None
     for source in range(CHIPS):
-        term = to_f32(r_mid[source]) * spread([grow[source, q : q + 1, :] for q in range(4)])
+        term = expand(to_f32(r_mid[source])) * spread([factor[source, q : q + 1, :] for q in range(4)])
         sums = term if sums is None else sums + term
     table[8:12] = sums.reshape(4, 8, BS)
-    def pack(first, count):
-        value = table[first : first + count]
-        scale = exponents(jnp.max(jnp.abs(value), axis=2, keepdims=True))
-        packed[first : first + count, :, :BS] = value * jnp.exp2(scale * -0.125)
-        packed[first : first + count, :, BS:] = jnp.broadcast_to(scale, (count, 8, 128))
-
-    pack(0, 16)
-    far.wait()
+    pack(0, 12)
+
+    collect(1, q_low, r_low)
+    sums = [None, None]
+    for source in range(CHIPS):
+        coded = to_f32(r_low[source])
+        scale = jnp.exp2(coded[64:80, :] * 0.125)
+        for h in range(2):
+            term = expand(coded[32 * h : 32 * h + 32, :]) * spread(
+                [scale[2 * q + h : 2 * q + h + 1, :] for q in (0, 1, 0, 1)]
+            )
+            sums[h] = term if sums[h] is None else sums[h] + term
+    table[12:16] = jnp.concatenate(sums, axis=1).reshape(4, 8, BS)
+    hop_down = pltpu.make_async_remote_copy(
+        src_ref=table.at[pl.ds(12, 4)], dst_ref=table.at[pl.ds(16, 4)],
+        send_sem=hop_send.at[1], recv_sem=hop_recv.at[1],
+        device_id=device(x, y, down, k), device_id_type=MESH,
+    )
+    hop_down.start()
+    pack(12, 4)
     hop_up.wait()
+    pack(20, 2)
     hop_down.wait()
-    pack(16, 6)
-
-    def code(reader, slot):
-        row = pairs_all[reader, 0, 0, slot]
-        col = pairs_all[reader, 1, 0, slot]
-        at = (row - z * BAND) * WIDTH + col - row + BAND - 1
-        return lookup[jnp.clip(at, 0, BAND * WIDTH - 1)]
-
-    def fill(o, px, py, pk):
-        slot = 2 * (((px % 2) * NY + py) * 2 + pk)
-        reader = px // 2
-        both = [packed[code(reader, slot + s) // 2] for s in range(2)]
+    pack(16, 4)
+
+    def fill(o):
+        both = [packed[codes[2 * o + s] // 2] for s in range(2)]
         stage[o] = to_i16(jnp.concatenate(both, axis=0))
 
     rank = k * CHIPS + me
@@ -394,41 +445,13 @@
         )
 
     def send_out(o, carry):
-        px, py, pk = plane_peer(o)
-        fill(o, px, py, pk)
+        fill(o)
         deliver(o).start()
         return carry
 
     lax.fori_loop(0, 2 * CHIPS - 1, send_out, 0)
-    fill(2 * CHIPS - 1, x, y, k)
+    fill(2 * CHIPS - 1)
     arrived[rank] = stage[2 * CHIPS - 1]
-
-    def take_out(o, carry):
-        px, py, pk = plane_peer(o)
-        source = pk * CHIPS + py * NX + px
-        pltpu.make_async_remote_copy(
-            src_ref=stage.at[o], dst_ref=arrived.at[source],
-            send_sem=out_send.at[o], recv_sem=out_recv.at[source],
-            device_id=device(px, py, z, pk), device_id_type=MESH,
-        ).wait_recv()
-        return carry
-
-    lax.fori_loop(0, 2 * CHIPS - 1, take_out, 0)
-    def unpack(source, carry):
-        value = to_f32(arrived[source])
-        scale = jnp.exp2(value[:, BS:] * 0.125)
-        value = value[:, :BS] * jnp.concatenate([scale, scale], axis=1)
-        blocks[0, source] = value[:8]
-        blocks[1, source] = value[8:]
-        return carry
-
-    lax.fori_loop(0, 2 * CHIPS, unpack, 0)
-    for s in range(2):
-        slot = 2 * token + s
-        block = blocks[s].reshape(BS, BS)
-        flip = code(c, slot) % 2 == 1
-        block = jnp.where(flip, block.T, block)
-        out_ref[0, s] = jnp.where(slot < counts_ref[0], block * weight, 0.0)
 
     for j in range(CHUNKS):
         x_copy(0, j).wait_send()
@@ -439,15 +462,13 @@
         swap_rows(g, 1).wait_send()
         swap_cols(g).wait_send()
         swap_below(g).wait_send()
-    swap_own.wait_send()
-    swap_ahead.wait_send()
     for o in range(1, NY):
         y_copy(o, y).wait_send()
     for o in range(1, NX):
         row_copy(o, x).wait_send()
     edge.wait_send()
     share_pairs.wait_send()
-    for g, got, land in ((0, q_mid, r_mid), (1, q_low, r_low)):
+    for g, got, land in ((0, q_mid, r_mid), (1, q_low, r_low), (2, q_edge, r_edge)):
         def left(o, carry):
             scatter_copy(g, got, land, o).wait_send()
             return carry
@@ -459,6 +480,34 @@
         return carry
 
     lax.fori_loop(0, 2 * CHIPS - 1, left_out, 0)
+
+    def unpack(source):
+        value = to_f32(arrived[source])
+        scale = jnp.exp2(value[:, BS:] * 0.125)
+        value = expand(value[:, :BS]) * jnp.concatenate([scale, scale], axis=1)
+        blocks[0, source] = value[:8]
+        blocks[1, source] = value[8:]
+
+    unpack(rank)
+
+    def take_out(o, carry):
+        px, py, pk = plane_peer(o)
+        source = pk * CHIPS + py * NX + px
+        pltpu.make_async_remote_copy(
+            src_ref=stage.at[o], dst_ref=arrived.at[source],
+            send_sem=out_send.at[o], recv_sem=out_recv.at[source],
+            device_id=device(px, py, z, pk), device_id_type=MESH,
+        ).wait_recv()
+        unpack(source)
+        return carry
+
+    lax.fori_loop(0, 2 * CHIPS - 1, take_out, 0)
+    for s in range(2):
+        slot = 2 * token + s
+        block = blocks[s].reshape(BS, BS)
+        flip = code(c, slot) % 2 == 1
+        block = jnp.where(flip, block.T, block)
+        out_ref[0, s] = jnp.where(slot < counts_ref[0], block * weight, 0.0)
 
 
 def shards(layer_input, pairs, counts):
@@ -477,13 +526,14 @@
         vmem((rows // 2, BS), bf16),
         vmem((rows // 2, columns), bf16),
         vmem((rows // 2, columns), bf16),
-        vmem((rows, BS // 2), bf16),
-        vmem((rows, BS), bf16),
         vmem((2, NY, NX, 24, BS), f32), vmem((NY, NX, 24, BS), f32),
-        vmem((NY, NX, 32, BS), f32), vmem((NY, NX, 40, BS), f32),
-        vmem((NY, NX, 32, BS), i16), vmem((NY, NX, 48, BS), i16), vmem((8, BS), f32),
-        vmem((NX, 24, BS), f32), vmem((CHIPS, 32, BS), i16), vmem((CHIPS, 48, BS), i16),
-        vmem((CHIPS, 8, BS), f32),
+        vmem((BS, rows), bf16), vmem((BS, columns), f32),
+        vmem((NY, NX, 32, BS), f32), vmem((NY, NX, 32, BS), f32),
+        vmem((2, NY, NX, 8, BS), f32), vmem((NY, NX, 8, BS), f32),
+        vmem((NY, NX, 32, BS), i16), vmem((NY, NX, 80, 128), i16), vmem((NY, NX, 16, BS), i16),
+        vmem((8, BS), f32), vmem((16, 128), f32), vmem((NX, 24, BS), f32),
+        vmem((CHIPS, 32, BS), i16), vmem((CHIPS, 80, 128), i16), vmem((CHIPS, 16, BS), i16),
+        vmem((72, BS), f32), vmem((CHIPS, 8, BS), f32),
     ]
     scratch += [
         vmem((22, 8, BS), f32),
@@ -494,14 +544,15 @@
         vmem(pairs.shape, jnp.int32),
         pltpu.SMEM((2,) + pairs.shape, jnp.int32),
         pltpu.SMEM((BAND * WIDTH,), jnp.int32),
+        pltpu.SMEM((4 * CHIPS,), jnp.int32),
         dma((3,)),
         dma((2, CHUNKS)), dma((2, CHUNKS)),
         dma((CHUNKS,)), dma((CHUNKS,)),
         dma, dma, dma, dma,
-        dma, dma, dma((4 * PARTS + 2,)), dma((4 * PARTS + 2,)),
+        dma((2,)), dma((2,)), dma((4 * PARTS,)), dma((4 * PARTS,)),
         vmem((NY, NX, 24, BS), f32), vmem((NX, 24, BS), f32),
         dma((NY,)), dma((NY,)), dma((NX,)), dma((NX,)),
-        dma((2, CHIPS)), dma((2, CHIPS)),
+        dma((3, CHIPS)), dma((3, CHIPS)),
         dma((2,)), dma((2,)),
         dma((2 * CHIPS,)), dma((2 * CHIPS,)),
     ]

time: 50.1 us -> 49.1 us (0.980)
  Pallas kernels: 48.5 us -> 47.5 us
    pallas_call x1, Pallas kernels: 48.5 us -> 47.5 us  [shards(): pl.pallas_call(functools.partial(kernel, weight), out_shape=jax.ShapeDtyp...]
where the time goes in v6:
time: 49.1 us; the launch traced here: 49 us
  Pallas kernels  47.5 us (97%)
  local copies, waits for them, and re-layouts  0.81 us (2%)
  between operations  0.68 us (1%)
    pallas_call x1, Pallas kernels, shards(): pl.pallas_call(functools.partial(kernel, weight), out_shape=jax.ShapeDtyp...  47.5 us

profile of v6, /device:TPU:1, one launch (start us, length us, event | category | flops | bytes accessed | tf_op | source)
XLA Modules:
  0.0 49.0 jit_solution(7311334331533499954)
XLA Ops:
  0.0 0.0 copy-start
  0.7 0.0 copy-done
  0.7 47.5 %shard_map.37 = f32[1,2,256,256]{3,2,1,0:T(8,128)S(1)} custom-call(bf16[1024,512]{1,0:T(8,128)(2,1)} %x_ref.1, s32[2,1,32]{2,1,0:T(1,128)S(1)} %copy-done, s32[1]{0:T(128)S(6)} %copy.5.counts_ref), custom_call_target="tpu_custom_call" | custom-call | tf_op jit(solution)/shard_map/pallas_call | solution.py:559
  48.2 0.8 %copy.6 = f32[1,2,256,256]{3,2,1,0:T(8,128)} copy(f32[1,2,256,256]{3,2,1,0:T(8,128)S(1)} %shard_map.37) | data formatting | bytes 1048576
Async XLA Ops:
  0.0 0.7 %copy-start = (s32[2,1,32]{2,1,0:T(1,128)S(1)}, s32[2,1,32]{2,1,0:T(1,128)}, u32[]{:S(2)}) copy-start(s32[2,1,32]{2,1,0:T(1,128)} %pairs_ref.1) | copy-start | bytes 772

commit v7 on v6

--- a/solution.py
+++ b/solution.py
@@ -202,14 +202,16 @@
         )
 
     def scatter(g, encode, got, land):
+        for row in range(NY):
+            for col in range(NX):
+                got[row, col] = encode(row, col)
+
         def send(o, carry):
-            px, py = chip_peer(o)
-            got[py, px] = encode(py, px)
             scatter_copy(g, got, land, o).start()
             return carry
 
         lax.fori_loop(0, CHIPS - 1, send, 0)
-        land[me] = encode(y, x)
+        land[me] = got[y, x]
 
     def collect(g, got, land):
         def take(o, carry):
@@ -261,22 +263,28 @@
             forward(j).wait_recv()
         swap_below(g).start()
 
+    def take_rows(g):
+        for j in range(g * per_part, (g + 1) * per_part):
+            x_arrival(0, j).wait_recv()
+        swap_rows(g, 0).start()
+        swap_rows(g, 1).start()
+        tokens = slice(g * part, (g + 1) * part)
+        near = [cross[0, tokens, pl.ds(pl.multiple_of(i * BS + k * (BS // 2), BS // 2), BS // 2)] for i in range(2)]
+        rows_t[:, tokens] = jnp.concatenate(near, axis=1).T
+
     for j in range(CHUNKS):
         x_arrival(1, j).wait_recv()
         forward(j).start()
-        x_arrival(0, j).wait_recv()
         if j == 0:
             own_along_y()
         if (j + 1) % per_part == 0:
             g = j // per_part
-            swap_rows(g, 0).start()
-            swap_rows(g, 1).start()
             swap_cols(g).start()
-            tokens = slice(g * part, (g + 1) * part)
-            near = [cross[0, tokens, pl.ds(pl.multiple_of(i * BS + k * (BS // 2), BS // 2), BS // 2)] for i in range(2)]
-            rows_t[:, tokens] = jnp.concatenate(near, axis=1).T
-            if g >= 2:
-                pass_below(g - 2)
+            if g >= 1:
+                take_rows(g - 1)
+    take_rows(PARTS - 1)
+    for g in range(PARTS - 2):
+        pass_below(g)
     share_pairs.wait_recv()
     load_pairs.wait()
     far = pltpu.make_async_copy(pairs_far, pairs_all.at[1 - c], local_sem.at[2])
@@ -288,12 +296,16 @@
         rows_t[:, half + g * part : half + (g + 1) * part] = far_rows[g * part : (g + 1) * part, :].T
         swap_cols(g).wait_recv()
 
+    def near_product(ref, first, last, cols):
+        return jnp.dot(rows_t[:, first:last], ref[first:last, cols], preferred_element_type=jnp.float32)
+
+    def far_product(ref, first, last, cols):
+        return jnp.dot(
+            rows_t[:, half + first : half + last], ref[first:last, cols], preferred_element_type=jnp.float32
+        )
+
     def product(near, far_part, first, last, cols):
-        return jnp.dot(
-            rows_t[:, first:last], near[first:last, cols], preferred_element_type=jnp.float32
-        ) + jnp.dot(
-            rows_t[:, half + first : half + last], far_part[first:last, cols], preferred_element_type=jnp.float32
-        )
+        return near_product(near, first, last, cols) + far_product(far_part, first, last, cols)
 
     def put_pairs(ref, j, both):
         put(ref, j, both[: BS // 2])
@@ -339,10 +351,13 @@
 
     scatter(2, encode_edge, q_edge, r_edge)
     pass_below(PARTS - 1)
+    for j in range(2):
+        cols = slice(j * BS, (j + 1) * BS)
+        sums_low[:, cols] = sums_low[:, cols] + near_product(below, early, half, cols)
     swap_below(PARTS - 1).wait_recv()
     for j in range(2):
         cols = slice(j * BS, (j + 1) * BS)
-        put_pairs(p_low, j, sums_low[:, cols] + product(below, far_below, early, half, cols))
+        put_pairs(p_low, j, sums_low[:, cols] + far_product(far_below, early, half, cols))
     rows = [exponents(jnp.maximum(peak(p_low, q), peak(p_low, 2 + q))) for q in range(2)]
     scales_low[...] = jnp.zeros_like(scales_low)
     for q in range(2):
@@ -444,13 +459,19 @@
             device_id=device(px, py, z, pk), device_id_type=MESH,
         )
 
-    def send_out(o, carry):
-        fill(o)
-        deliver(o).start()
+    def send_out(i, carry):
+        for u in range(4):
+            fill(4 * i + u)
+        for u in range(4):
+            deliver(4 * i + u).start()
         return carry
 
-    lax.fori_loop(0, 2 * CHIPS - 1, send_out, 0)
-    fill(2 * CHIPS - 1)
+    groups = 2 * CHIPS // 4
+    lax.fori_loop(0, groups - 1, send_out, 0)
+    for u in range(4):
+        fill(4 * (groups - 1) + u)
+    for u in range(3):
+        deliver(4 * (groups - 1) + u).start()
     arrived[rank] = stage[2 * CHIPS - 1]
 
     for j in range(CHUNKS):
@@ -488,8 +509,6 @@
         blocks[0, source] = value[:8]
         blocks[1, source] = value[8:]
 
-    unpack(rank)
-
     def take_out(o, carry):
         px, py, pk = plane_peer(o)
         source = pk * CHIPS + py * NX + px
@@ -498,10 +517,16 @@
             send_sem=out_send.at[o], recv_sem=out_recv.at[source],
             device_id=device(px, py, z, pk), device_id_type=MESH,
         ).wait_recv()
-        unpack(source)
         return carry
 
     lax.fori_loop(0, 2 * CHIPS - 1, take_out, 0)
+
+    def unpack_four(i, carry):
+        for u in range(4):
+            unpack(4 * i + u)
+        return carry
+
+    lax.fori_loop(0, groups, unpack_four, 0)
     for s in range(2):
         slot = 2 * token + s
         block = blocks[s].reshape(BS, BS)

time: 49.1 us -> 49.2 us (level)
  no operation moved by 1% of the time
where the time goes in v7:
time: 49.2 us; the launch traced here: 49.1 us
  Pallas kernels  47.6 us (97%)
  local copies, waits for them, and re-layouts  0.81 us (2%)
  between operations  0.68 us (1%)
    pallas_call x1, Pallas kernels, shards(): pl.pallas_call(functools.partial(kernel, weight), out_shape=jax.ShapeDtyp...  47.6 us

profile of v7, /device:TPU:1, one launch (start us, length us, event | category | flops | bytes accessed | tf_op | source)
XLA Modules:
  0.0 49.1 jit_solution(1216682084708272417)
XLA Ops:
  0.0 0.0 copy-start
  0.7 0.0 copy-done
  0.7 47.6 %shard_map.37 = f32[1,2,256,256]{3,2,1,0:T(8,128)S(1)} custom-call(bf16[1024,512]{1,0:T(8,128)(2,1)} %x_ref.1, s32[2,1,32]{2,1,0:T(1,128)S(1)} %copy-done, s32[1]{0:T(128)S(6)} %copy.5.counts_ref), custom_call_target="tpu_custom_call" | custom-call | tf_op jit(solution)/shard_map/pallas_call | solution.py:584
  48.3 0.8 %copy.6 = f32[1,2,256,256]{3,2,1,0:T(8,128)} copy(f32[1,2,256,256]{3,2,1,0:T(8,128)S(1)} %shard_map.37) | data formatting | bytes 1048576
Async XLA Ops:
  0.0 0.7 %copy-start = (s32[2,1,32]{2,1,0:T(1,128)S(1)}, s32[2,1,32]{2,1,0:T(1,128)}, u32[]{:S(2)}) copy-start(s32[2,1,32]{2,1,0:T(1,128)} %pairs_ref.1) | copy-start | bytes 772

commit v8 on v7

--- a/solution.py
+++ b/solution.py
@@ -460,18 +460,17 @@
         )
 
     def send_out(i, carry):
-        for u in range(4):
-            fill(4 * i + u)
-        for u in range(4):
-            deliver(4 * i + u).start()
+        for u in range(2):
+            fill(2 * i + u)
+        for u in range(2):
+            deliver(2 * i + u).start()
         return carry
 
     groups = 2 * CHIPS // 4
-    lax.fori_loop(0, groups - 1, send_out, 0)
-    for u in range(4):
-        fill(4 * (groups - 1) + u)
-    for u in range(3):
-        deliver(4 * (groups - 1) + u).start()
+    lax.fori_loop(0, CHIPS - 1, send_out, 0)
+    fill(2 * CHIPS - 2)
+    deliver(2 * CHIPS - 2).start()
+    fill(2 * CHIPS - 1)
     arrived[rank] = stage[2 * CHIPS - 1]
 
     for j in range(CHUNKS):

time: 49.2 us -> 49.1 us (level)
  no operation moved by 1% of the time
where the time goes in v8:
time: 49.1 us; the launch traced here: 48.9 us
  Pallas kernels  47.5 us (97%)
  local copies, waits for them, and re-layouts  0.81 us (2%)
  between operations  0.68 us (1%)
    pallas_call x1, Pallas kernels, shards(): pl.pallas_call(functools.partial(kernel, weight), out_shape=jax.ShapeDtyp...  47.5 us

profile of v8, /device:TPU:1, one launch (start us, length us, event | category | flops | bytes accessed | tf_op | source)
XLA Modules:
  0.0 48.9 jit_solution(6949717409355640323)
XLA Ops:
  0.0 0.0 copy-start
  0.7 0.0 copy-done
  0.7 47.5 %shard_map.37 = f32[1,2,256,256]{3,2,1,0:T(8,128)S(1)} custom-call(bf16[1024,512]{1,0:T(8,128)(2,1)} %x_ref.1, s32[2,1,32]{2,1,0:T(1,128)S(1)} %copy-done, s32[1]{0:T(128)S(6)} %copy.5.counts_ref), custom_call_target="tpu_custom_call" | custom-call | tf_op jit(solution)/shard_map/pallas_call | solution.py:583
  48.1 0.8 %copy.6 = f32[1,2,256,256]{3,2,1,0:T(8,128)} copy(f32[1,2,256,256]{3,2,1,0:T(8,128)S(1)} %shard_map.37) | data formatting | bytes 1048576
Async XLA Ops:
  0.0 0.7 %copy-start = (s32[2,1,32]{2,1,0:T(1,128)S(1)}, s32[2,1,32]{2,1,0:T(1,128)}, u32[]{:S(2)}) copy-start(s32[2,1,32]{2,1,0:T(1,128)} %pairs_ref.1) | copy-start | bytes 772
